TPU v7x, 32 devices: a whole 2x2x4 slice. The times are simulated.
32 devices in a mesh: dp: 16 (over z, x, core), expert: 2 (over y).
Axes of the slice: x: 2, y: 2, z: 4, core: 2. Of those that a mesh axis runs over, the one named last changes fastest.
Arguments:
- tokens: bfloat16 [4096, 3584], P(('dp', 'expert')), may hold values from -6 to 6
- cotangent: bfloat16 [4096, 3584], P(('dp', 'expert')), may hold values from -6 to 6
- experts: int32 [4096, 2], P(('dp', 'expert')), may hold values from 0 to 63, all different within a row
- route_weight: float32 [4096, 2], P(('dp', 'expert')), may hold values from 0.05 to 1
- w_gate: bfloat16 [2, 7168, 3584], P('expert', 'dp'), may hold values from -0.09375 to 0.09375
- w_up: bfloat16 [2, 7168, 3584], P('expert', 'dp'), may hold values from -0.09375 to 0.09375
- w_down: bfloat16 [2, 7168, 3584], P('expert', 'dp'), may hold values from -0.0625 to 0.0625
Outputs:
- token_grad: bfloat16 [4096, 3584], P(('dp', 'expert'))
- grad_gate: bfloat16 [2, 7168, 3584], P('expert', 'dp')
- grad_up: bfloat16 [2, 7168, 3584], P('expert', 'dp')
- grad_down: bfloat16 [2, 7168, 3584], P('expert', 'dp')
Inputs may be any that keep to these rules, and one draw needn't show every extreme that they name: Each token names 2 different experts of the 64.
All inputs are finite; a program needn't handle non-finite values.
Results may differ from a plain program's by a relative error of at most 0.024.
Values may be sent and summed in bfloat16 or wider, within the bound.
A program may use at most 128 MiB of HBM per device.

v0:
```python
import jax
import jax.numpy as jnp
from jax import lax
from jax.sharding import PartitionSpec as P

CAP = 4


def slot_table(experts_local, window, capacity):
    flat = experts_local.reshape(-1)
    count = flat.shape[0]
    labels = jnp.arange(window, dtype=jnp.int32)
    onehot = (flat[:, None] == labels[None, :]).astype(jnp.int32)
    before = jnp.cumsum(onehot, axis=0) - onehot
    slot = jnp.sum(before * onehot, axis=1)
    keep = (jnp.sum(onehot, axis=1) > 0) & (slot < capacity)
    target = jnp.where(keep, flat * capacity + slot, -1)
    places = jnp.arange(window * capacity, dtype=jnp.int32)
    match = (target[None, :] == places[:, None]).astype(jnp.int32)
    source = jnp.sum(match * jnp.arange(count, dtype=jnp.int32)[None, :], axis=1)
    filled = jnp.sum(match, axis=1) > 0
    return (flat, slot, keep, source, filled)


def expert_terms(x_rows, c_rows, gate_w, up_w, down_w):
    gate = jnp.einsum("rd,fd->rf", x_rows, gate_w, preferred_element_type=jnp.float32)
    up = jnp.einsum("rd,fd->rf", x_rows, up_w, preferred_element_type=jnp.float32)
    sig = jax.nn.sigmoid(gate)
    act = gate * sig
    hidden = (act * up).astype(jnp.bfloat16)
    back = jnp.einsum("rd,fd->rf", c_rows, down_w, preferred_element_type=jnp.float32)
    d_gate = (back * up * sig * (1.0 + gate * (1.0 - sig))).astype(jnp.bfloat16)
    d_up = (back * act).astype(jnp.bfloat16)
    return (hidden, d_gate, d_up)


def weight_terms(x_rows, c_rows, hidden, d_gate, d_up):
    grad_g = jnp.einsum("rf,rd->fd", d_gate, x_rows, preferred_element_type=jnp.float32)
    grad_u = jnp.einsum("rf,rd->fd", d_up, x_rows, preferred_element_type=jnp.float32)
    grad_d = jnp.einsum("rf,rd->fd", hidden, c_rows, preferred_element_type=jnp.float32)
    return (grad_g, grad_u, grad_d)


def shards(tokens, cotangent, experts, route_weight, w_gate, w_up, w_down):
    window = lax.axis_size("expert")
    top = experts.shape[1]
    width = tokens.shape[1]
    capacity = CAP
    gate_w = w_gate[0]
    up_w = w_up[0]
    down_w = w_down[0]
    flat, slot, keep, source, filled = slot_table(experts, window, capacity)
    which = source // top
    x_slots = jnp.where(filled[:, None], tokens[which], jnp.zeros((), tokens.dtype))
    scaled = route_weight.reshape(-1)[source][:, None] * cotangent[which].astype(jnp.float32)
    c_slots = jnp.where(filled[:, None], scaled, jnp.float32(0.0)).astype(jnp.bfloat16)
    x_slots = x_slots.reshape(window, capacity, width)
    c_slots = c_slots.reshape(window, capacity, width)
    arrived = (
        lax.all_to_all(x_slots, "expert", split_axis=0, concat_axis=0, tiled=True),
        lax.all_to_all(c_slots, "expert", split_axis=0, concat_axis=0, tiled=True),
    )
    x_whole, c_whole = (
        lax.all_gather(arrived[0], "dp", axis=0, tiled=True),
        lax.all_gather(arrived[1], "dp", axis=0, tiled=True),
    )
    x_rows = x_whole.reshape(-1, width)
    c_rows = c_whole.reshape(-1, width)
    hidden_all, d_gate_all, d_up_all = expert_terms(x_rows, c_rows, gate_w, up_w, down_w)
    grad_g, grad_u, grad_d = weight_terms(x_rows, c_rows, hidden_all, d_gate_all, d_up_all)
    terms = jnp.einsum(
        "rf,fd->rd", d_gate_all, gate_w, preferred_element_type=jnp.float32
    ) + jnp.einsum("rf,fd->rd", d_up_all, up_w, preferred_element_type=jnp.float32)
    summed = lax.psum_scatter(terms.astype(jnp.bfloat16), "dp", scatter_dimension=0, tiled=True)
    slot_grad = summed.reshape(window, capacity, width)
    returned = lax.all_to_all(slot_grad, "expert", split_axis=0, concat_axis=0, tiled=True).reshape(
        window * capacity, width
    )
    index = jnp.where(keep, flat * capacity + slot, 0)
    picked = jnp.where(keep[:, None], returned[index].astype(jnp.float32), jnp.float32(0.0))
    token_grad = picked.reshape(-1, top, width).sum(axis=1).astype(jnp.bfloat16)
    return (
        token_grad,
        grad_g.astype(jnp.bfloat16)[None],
        grad_u.astype(jnp.bfloat16)[None],
        grad_d.astype(jnp.bfloat16)[None],
    )


def solution(mesh):
    in_specs = (
        P(("dp", "expert"), None),
        P(("dp", "expert"), None),
        P(("dp", "expert"), None),
        P(("dp", "expert"), None),
        P("expert", "dp", None),
        P("expert", "dp", None),
        P("expert", "dp", None),
    )
    out_specs = (
        P(("dp", "expert"), None),
        P("expert", "dp", None),
        P("expert", "dp", None),
        P("expert", "dp", None),
    )
    return jax.shard_map(shards, mesh=mesh, in_specs=in_specs, out_specs=out_specs, check_vma=False)
```

profile of v0, /device:TPU:0, one launch (start us, length us, event | category | flops | bytes accessed | tf_op | source)
XLA Modules:
  0.0 176.4 jit_solution(10470138087440980397)
XLA Ops:
  10.9 1.9 %gather_fusion.1 = bf16[8,3584]{1,0:T(8,128)(2,1)S(1)} fusion(bf16[128,3584]{1,0:T(8,128)(2,1)} %param.8, s32[1024]{0:T(1024)S(1)} %get-tuple-element.14), kind=kCustom, calls=%fused_computation.1 | custom fusion | bytes 114720 | tf_op jit(solution)/shard_map/gather | solution.py:55
  15.3 4.2 %all-to-all-start = ((bf16[2,4,3584]{2,1,0:T(4,128)(2,1)}), bf16[2,4,3584]{2,1,0:T(4,128)(2,1)S(1)}, u32[]{:S(2)}, u32[]{:S(2)}) async-start(bf16[2,4,3584]{2,1,0:T(4,128)(2,1)} %select_convert_fusion), calls=%async_computation | async-start | bytes 114688 | tf_op jit(solution)/shard_map/all_to_all | solution.py:61
  19.5 1.9 %gather_fusion.2 = bf16[8,3584]{1,0:T(8,128)(2,1)S(1)} fusion(bf16[128,3584]{1,0:T(8,128)(2,1)} %param.7, s32[1024]{0:T(1024)S(1)} %get-tuple-element.14), kind=kCustom, calls=%fused_computation.2 | custom fusion | bytes 114720 | tf_op jit(solution)/shard_map/gather | solution.py:54
  22.2 1.4 all-to-all-done
  23.6 3.3 %all-to-all-start.1 = ((bf16[2,4,3584]{2,1,0:T(4,128)(2,1)}), bf16[2,4,3584]{2,1,0:T(4,128)(2,1)S(1)}, u32[]{:S(2)}, u32[]{:S(2)}) async-start(bf16[2,4,3584]{2,1,0:T(4,128)(2,1)} %broadcast_select_fusion), calls=%async_computation.1 | async-start | bytes 114688 | tf_op jit(solution)/shard_map/all_to_all | solution.py:60
  27.0 26.2 %all_gather.6 = bf16[32,4,3584]{2,1,0:T(4,128)(2,1)} all-gather(bf16[2,4,3584]{2,1,0:T(4,128)(2,1)S(1)} %all-to-all-done), channel_id=1, replica_groups=mesh['dp'=16,'expert'=2] {'dp'}, dimensions={0}, use_global_device_ids=true | all-gather | bytes 974848 | tf_op jit(solution)/shard_map/all_gather | solution.py:65
  53.1 2.4 %reshape.219 = bf16[128,3584]{1,0:T(8,128)(2,1)} reshape(bf16[32,4,3584]{2,1,0:T(4,128)(2,1)} %all_gather.6) | data formatting | bytes 1835008 | tf_op jit(solution)/shard_map/reshape | solution.py:68
  55.5 21.4 %all_gather.7 = bf16[32,4,3584]{2,1,0:T(4,128)(2,1)} all-gather(bf16[2,4,3584]{2,1,0:T(4,128)(2,1)S(1)} %all-to-all-done.1), channel_id=1, replica_groups=mesh['dp'=16,'expert'=2] {'dp'}, dimensions={0}, use_global_device_ids=true | all-gather | bytes 974848 | tf_op jit(solution)/shard_map/all_gather | solution.py:64
  76.9 2.4 %reshape.220 = bf16[128,3584]{1,0:T(8,128)(2,1)} reshape(bf16[32,4,3584]{2,1,0:T(4,128)(2,1)} %all_gather.7) | data formatting | bytes 1835008 | tf_op jit(solution)/shard_map/reshape | solution.py:67
  79.3 2.3 %fusion.6 = f32[128,448]{0,1:T(8,128)S(1)} fusion(bf16[128,3584]{1,0:T(8,128)(2,1)} %reshape.220, bf16[1,448,3584]{2,1,0:T(8,128)(2,1)S(1)} %copy-done), kind=kOutput, calls=%fused_computation.15 | convolution fusion | flops 411041792 | bytes 4358144 | tf_op jit(solution)/shard_map/rd,fd->rf/dot_general | solution.py:26
  85.7 1.6 fusion.3
  87.3 1.3 broadcast_multiply_fusion
  88.6 1.4 copy.22
  90.0 1.6 mul.77
  91.6 1.4 and.42
  94.4 3.9 %fusion.1 = bf16[1,448,3584]{2,1,0:T(8,128)(2,1)} fusion(bf16[128,448]{0,1:T(8,128)(2,1)} %copy-done.7, bf16[128,3584]{1,0:T(8,128)(2,1)} %reshape.220), kind=kOutput, calls=%fused_computation.8 | convolution fusion | flops 412647424 | bytes 4243456 | tf_op jit(solution)/shard_map/rf,rd->fd/dot_general | solution.py:39
  98.3 2.7 %fusion.2 = bf16[1,448,3584]{2,1,0:T(8,128)(2,1)} fusion(bf16[128,3584]{1,0:T(8,128)(2,1)S(1)} %copy-done.4, f32[128,448]{0,1:T(8,128)S(1)} %copy-done.6, f32[128,448]{0,1:T(8,128)S(1)} %fusion.6), kind=kOutput, calls=%fused_computation.9 | convolution fusion | flops 412991488 | bytes 4587520 | tf_op jit(solution)/shard_map/rf,rd->fd/dot_general | solution.py:40
  101.0 42.7 %reduce-scatter.2.cloned.1.call-done = bf16[8,3584]{1,0:T(8,128)(2,1)} async-done(((bf16[128,3584]{1,0:T(8,128)(2,1)}), bf16[8,3584]{1,0:T(8,128)(2,1)}) %reduce-scatter.2.cloned.1.call-update) | async-done | bytes 57360 | tf_op jit(solution)/shard_map/reduce_scatter | solution.py:74
  143.7 1.5 reshape.221
  145.1 3.5 %all-to-all-start.2 = ((bf16[2,4,3584]{2,1,0:T(4,128)(2,1)}), bf16[2,4,3584]{2,1,0:T(4,128)(2,1)S(1)}, u32[]{:S(2)}, u32[]{:S(2)}) async-start(bf16[2,4,3584]{2,1,0:T(4,128)(2,1)} %reshape.221), calls=%async_computation.3 | async-start | bytes 114688 | tf_op jit(solution)/shard_map/all_to_all | solution.py:76
  148.6 3.8 %fusion = bf16[1,448,3584]{2,1,0:T(8,128)(2,1)} fusion(bf16[128,448]{0,1:T(8,128)(2,1)S(1)} %get-tuple-element.11, bf16[128,3584]{1,0:T(8,128)(2,1)} %reshape.220), kind=kOutput, calls=%fused_computation.7 | convolution fusion | flops 412647424 | bytes 4243456 | tf_op jit(solution)/shard_map/rf,rd->fd/dot_general | solution.py:38
  152.5 3.1 %gather_fusion.3 = bf16[256,3584]{1,0:T(8,128)(2,1)} fusion(bf16[8,3584]{1,0:T(8,128)(2,1)S(1)} %reshape.222, s32[1024]{0:T(1024)} %pad_clamp_fusion), kind=kCustom, calls=%fused_computation.3 | custom fusion | bytes 3671040 | tf_op jit(solution)/shard_map/gather | solution.py:80
  155.6 5.2 %reshape.224 = f32[128,2,3584]{2,1,0:T(2,128)} reshape(bf16[256,3584]{1,0:T(8,128)(2,1)} %gather_fusion.3) | data formatting | bytes 5505024 | tf_op jit(solution)/shard_map/convert_element_type | solution.py:80
  160.8 8.8 %select_reduce_fusion = bf16[128,3584]{1,0:T(8,128)(2,1)} fusion(f32[128,2,3584]{2,1,0:T(2,128)} %reshape.224, pred[128,2]{1,0:T(8,128)(4,1)S(1)} %copy-done.8), kind=kLoop, calls=%fused_computation.12 | loop fusion | flops 1376256 | bytes 4587776 | tf_op jit(solution)/shard_map/reduce_sum | solution.py:81
  (58 shorter events, 12.4 us)
Async XLA Ops:
  7.2 72.2 %copy-start = (bf16[1,448,3584]{2,1,0:T(8,128)(2,1)S(1)}, bf16[1,448,3584]{2,1,0:T(8,128)(2,1)}, u32[]{:S(2)}) copy-start(bf16[1,448,3584]{2,1,0:T(8,128)(2,1)} %param.11) | copy-start | bytes 9633796
  9.5 0.6 copy-start.9
  10.1 0.6 copy-start.10
  15.3 8.3 %all-to-all-start = ((bf16[2,4,3584]{2,1,0:T(4,128)(2,1)}), bf16[2,4,3584]{2,1,0:T(4,128)(2,1)S(1)}, u32[]{:S(2)}, u32[]{:S(2)}) async-start(bf16[2,4,3584]{2,1,0:T(4,128)(2,1)} %select_convert_fusion), calls=%async_computation | async-start | bytes 114688 | tf_op jit(solution)/shard_map/all_to_all | solution.py:61
  23.6 31.9 %all-to-all-start.1 = ((bf16[2,4,3584]{2,1,0:T(4,128)(2,1)}), bf16[2,4,3584]{2,1,0:T(4,128)(2,1)S(1)}, u32[]{:S(2)}, u32[]{:S(2)}) async-start(bf16[2,4,3584]{2,1,0:T(4,128)(2,1)} %broadcast_select_fusion), calls=%async_computation.1 | async-start | bytes 114688 | tf_op jit(solution)/shard_map/all_to_all | solution.py:60
  26.9 116.8 %reduce-scatter.2.cloned.1.call-start = ((), (), s32[]{:S(2)}) async-start(), calls=%async_computation.4 | async-start | bytes 974848 | tf_op jit(solution)/shard_map/reduce_scatter | solution.py:74
  79.3 2.3 %copy-start.1 = (bf16[128,3584]{1,0:T(8,128)(2,1)S(1)}, bf16[128,3584]{1,0:T(8,128)(2,1)}, u32[]{:S(2)}) copy-start(bf16[128,3584]{1,0:T(8,128)(2,1)} %reshape.220) | copy-start | bytes 2752516
  79.3 2.5 %copy-start.2 = (bf16[1,448,3584]{2,1,0:T(8,128)(2,1)S(1)}, bf16[1,448,3584]{2,1,0:T(8,128)(2,1)}, u32[]{:S(2)}) copy-start(bf16[1,448,3584]{2,1,0:T(8,128)(2,1)} %param.12) | copy-start | bytes 9633796
  81.8 1.2 copy-start.3
  81.8 2.2 %copy-start.11 = (bf16[1,448,3584]{2,1,0:T(8,128)(2,1)S(1)}, bf16[1,448,3584]{2,1,0:T(8,128)(2,1)}, u32[]{:S(2)}) copy-start(bf16[1,448,3584]{2,1,0:T(8,128)(2,1)} %param.13) | copy-start | bytes 9633796
  84.0 1.7 copy-start.5
  85.0 0.7 copy-start.7
  93.0 5.3 %copy-start.4 = (bf16[128,3584]{1,0:T(8,128)(2,1)S(1)}, bf16[128,3584]{1,0:T(8,128)(2,1)}, u32[]{:S(2)}) copy-start(bf16[128,3584]{1,0:T(8,128)(2,1)} %reshape.219) | copy-start | bytes 2752516
  93.0 5.3 %copy-start.6 = (f32[128,448]{0,1:T(8,128)S(1)}, f32[128,448]{0,1:T(8,128)}, u32[]{:S(2)}) copy-start(f32[128,448]{0,1:T(8,128)} %copy-done.5) | copy-start | bytes 688132
  145.1 7.4 %all-to-all-start.2 = ((bf16[2,4,3584]{2,1,0:T(4,128)(2,1)}), bf16[2,4,3584]{2,1,0:T(4,128)(2,1)S(1)}, u32[]{:S(2)}, u32[]{:S(2)}) async-start(bf16[2,4,3584]{2,1,0:T(4,128)(2,1)} %reshape.221), calls=%async_computation.3 | async-start | bytes 114688 | tf_op jit(solution)/shard_map/all_to_all | solution.py:76
  155.6 5.2 %copy-start.8 = (pred[128,2]{1,0:T(8,128)(4,1)S(1)}, pred[128,2]{1,0:T(8,128)(4,1)}, u32[]{:S(2)}) copy-start(pred[128,2]{1,0:T(8,128)(4,1)} %and.42) | copy-start | bytes 772
Sparse Core Ops, SparseCore 0:
  87.4 56.2 reduce-scatter.1
where the time goes:
time: 177 us; the launch traced here: 176 us
  blocking collectives  47.6 us (27%)
  waiting for transfers between devices  44.2 us (25%)
  local copies, waits for them, and re-layouts  27.9 us (16%)
  matrix products  17 us (10%)
  other arithmetic  14.5 us (8%)
  between operations  14.2 us (8%)
  starting transfers between devices  11 us (6%)
    reduce_scatter x1, waiting for transfers between devices, shards(): lax.psum_scatter(terms.astype(jnp.bfloat16), 'dp', scatter_dimension=0, t...  42.7 us
    all_gather x1, blocking collectives, shards(): lax.all_gather(arrived[1], 'dp', axis=0, tiled=True)  26.2 us
    all_gather x1, blocking collectives, shards(): lax.all_gather(arrived[0], 'dp', axis=0, tiled=True)  21.4 us
    reduce_sum x1, other arithmetic, shards(): token_grad = picked.reshape(-1, top, width).sum(axis=1).astype(jnp.bfloat16)  8.78 us
    convert_element_type x1, local copies, waits for them, and re-layouts, shards(): returned[index].astype(jnp.float32)  5.2 us
    all_to_all x1, starting transfers between devices, shards(): lax.all_to_all(c_slots, 'expert', split_axis=0, concat_axis=0, tiled=True)  4.23 us
    dot_general x1, matrix products, weight_terms(): jnp.einsum('rf,rd->fd', d_up, x_rows, preferred_element_type=jnp.float32)  3.93 us
    dot_general x1, matrix products, weight_terms(): jnp.einsum('rf,rd->fd', d_gate, x_rows, preferred_element_type=jnp.float32)  3.85 us
  transfers between devices with their start and end apart: 4, of which 2 were waited for; matrix products, arithmetic and copies ran while one was open for 13% of the time, Pallas kernels for 0%

commit v1 on v0

v1 whole, which is shorter than its diff:
```python
import functools

import jax
import jax.numpy as jnp
import numpy as np
from jax import lax
from jax.experimental import pallas as pl
from jax.experimental.pallas import tpu as pltpu
from jax.sharding import PartitionSpec as P

CAP = 4
MESH = pl.DeviceIdType.MESH
F32 = jnp.float32
BF16 = jnp.bfloat16
NT = (((1,), (1,)), ((), ()))


def one_hots(experts, place_expert, place_slot):
    count = experts.shape[0]
    first = experts[:, 0:1] == place_expert
    second = experts[:, 1:2] == place_expert
    named = jnp.where(first | second, 1.0, 0.0).astype(F32)
    shape = (count, count)
    earlier = lax.broadcasted_iota(jnp.int32, shape, 1) < lax.broadcasted_iota(jnp.int32, shape, 0)
    earlier = jnp.where(earlier, 1.0, 0.0).astype(BF16)
    before = jnp.dot(earlier, named.astype(BF16), preferred_element_type=F32)
    return jnp.where(before == place_slot.astype(F32), named, 0.0), first


def exchange_kernel(
    n_dp, window,
    tokens, cotangent, experts, weights, select, w_gate, w_up, w_down,
    rows_out, d_out, back_out, pick_out,
    w, sent, arrived, rows, prod, d_rows, part, sib, out_buf, in_buf,
    w_sem, y_send, y_recv, ring_send, ring_recv, sib_send, sib_recv,
    pair_send, pair_recv, rs_send, rs_recv, z_send, z_recv, local_sem,
):
    width = tokens.shape[1]
    half = width // 2
    quarter = half // 2
    hidden = w_gate.shape[0]
    chips = n_dp // 2
    far = chips // 2
    group = 2 * CAP
    kept = window * CAP
    block = window * group
    total = n_dp * block

    me = lax.axis_index("dp")
    mine = lax.axis_index("expert")
    core = lax.rem(me, 2)
    chip = lax.div(me, 2)
    spot = jnp.where(lax.rem(chip, 2) == 0, lax.div(chip, 2), chips - 1 - lax.div(chip, 2))

    def chip_at(place):
        place = lax.rem(place + 2 * chips, chips)
        return jnp.where(place < far, 2 * place, 2 * (chips - 1 - place) + 1)

    def at(place):
        return 2 * chip_at(place) + core

    sibling = (2 * chip + 1 - core, mine)
    neighbour = ((at(spot + 1), mine), (at(spot - 1), mine))

    loads = []
    for index, source in enumerate((w_gate, w_up, w_down)):
        loads.append(pltpu.make_async_copy(source, w.at[pl.ds(index * hidden, hidden), :], w_sem.at[index]))
        loads[-1].start()

    barrier = pltpu.get_barrier_semaphore()
    greet = [sibling, *neighbour]
    for step in range(1, window):
        greet.append((me, lax.rem(mine + step, window)))
    for device in greet:
        pl.semaphore_signal(barrier, inc=1, device_id=device, device_id_type=MESH)

    lanes = max(128, block)
    place = lax.broadcasted_iota(jnp.int32, (1, lanes), 1)
    match, first = one_hots(experts[...], lax.div(place, group), lax.rem(place, CAP))
    match_t = jnp.transpose(match)[:block]
    scale = jnp.transpose(jnp.where(first, weights[:, 0:1], weights[:, 1:2]) * match)[:block]
    scale = jnp.sum(scale, axis=1, keepdims=True)
    is_x = lax.rem(lax.broadcasted_iota(jnp.int32, match_t.shape, 0), group) < CAP
    slots = jnp.dot(jnp.where(is_x, match_t, 0.0).astype(BF16), tokens[...], preferred_element_type=F32)
    slots += scale * jnp.dot(
        jnp.where(is_x, 0.0, match_t).astype(BF16), cotangent[...], preferred_element_type=F32
    )
    for e in range(window):
        piece = slots[e * group:(e + 1) * group]
        sent[e] = jnp.concatenate([piece[:, :half], piece[:, half:]], axis=0).astype(BF16)

    pl.semaphore_wait(barrier, len(greet))

    swaps = []
    for step in range(1, window):
        other = lax.rem(mine + step, window)
        swaps.append(pltpu.make_async_remote_copy(
            src_ref=sent.at[other], dst_ref=arrived.at[mine],
            send_sem=y_send.at[step], recv_sem=y_recv.at[step],
            device_id=(me, other), device_id_type=MESH,
        ))
        swaps[-1].start()
    arrived[mine] = sent[mine]

    columns = window * 2 * kept
    place = lax.broadcasted_iota(jnp.int32, (1, columns), 1)
    row = lax.rem(place, kept)
    match, _ = one_hots(experts[...], lax.div(place, 2 * kept), lax.rem(row, CAP))
    match = jnp.where(lax.div(row, CAP) == mine, match, 0.0)
    side = lax.rem(lax.div(place, kept), 2)
    for h in range(2):
        pick_out[h] = jnp.where(side == h, match, 0.0).astype(BF16)

    for copy in swaps:
        copy.wait_recv()
    for h in range(2):
        own = [arrived[s].astype(F32)[h * group:(h + 1) * group] for s in range(window)]
        rows[me, :, pl.ds(h * half, half)] = jnp.concatenate(own, axis=0).astype(BF16)

    def hop(way, step, h):
        origin = at(spot - step) if way == 0 else at(spot + step)
        view = rows.at[origin, :, pl.ds(h * half, half)]
        return pltpu.make_async_remote_copy(
            src_ref=view, dst_ref=view,
            send_sem=ring_send.at[way, step, h], recv_sem=ring_recv.at[way, step, h],
            device_id=neighbour[way], device_id_type=MESH,
        )

    def share(way, step, h):
        origin = at(spot - step) if way == 0 else at(spot + step)
        view = rows.at[origin, :, pl.ds(h * half, half)]
        return pltpu.make_async_remote_copy(
            src_ref=view, dst_ref=view,
            send_sem=sib_send.at[way, step, h], recv_sem=sib_recv.at[way, step, h],
            device_id=sibling, device_id_type=MESH,
        )

    def travels(way, step, h):
        return step < far - 1 or (step == far - 1 and way == h)

    hops, shares = [], []
    for h in range(2):
        for way in range(2):
            hops.append(hop(way, 0, h))
            hops[-1].start()
    for h in range(2):
        shares.append(share(0, 0, h))
        shares[-1].start()
    for step in range(far):
        for h in range(2):
            for way in range(2):
                if travels(way, step, h):
                    hop(way, step, h).wait_recv()
                    if travels(way, step + 1, h):
                        hops.append(hop(way, step + 1, h))
                        hops[-1].start()
                    shares.append(share(way, step + 1, h))
                    shares[-1].start()
    for copy in loads:
        copy.wait()
    for copy in shares:
        copy.wait_recv()
    gathered = pltpu.make_async_copy(rows, rows_out, local_sem)
    gathered.start()

    wide = 256 if total % 256 == 0 else total
    deep = 512
    blocks = wide // block
    tall = 32

    def products(n, carry):
        start = pl.multiple_of(n * wide, wide)

        def chunk(k, carry):
            at_k = pl.ds(pl.multiple_of(k * deep, deep), deep)
            piece = rows[pl.ds(n * blocks, blocks), :, at_k].reshape(wide, deep)
            term = lax.dot_general(w[:, at_k], piece, NT, preferred_element_type=F32)

            @pl.when(k == 0)
            def _():
                prod[...] = term

            @pl.when(k > 0)
            def _():
                prod[...] += term

            return carry

        lax.fori_loop(0, width // deep, chunk, 0)

        def pointwise(i, carry):
            def rows_of(index):
                return pl.ds(pl.multiple_of(index * hidden + i * tall, tall), tall)

            gate = prod[rows_of(0), :]
            up = prod[rows_of(1), :]
            back = pltpu.roll(prod[rows_of(2), :], wide - CAP, 1)
            sig = jax.nn.sigmoid(gate)
            act = gate * sig
            lane = lax.broadcasted_iota(jnp.int32, gate.shape, 1)
            is_x = lax.rem(lane, group) < CAP
            hid = pltpu.roll(act * up, CAP, 1)
            d_gate = back * up * sig * (1.0 + gate * (1.0 - sig))
            d_up = back * act
            cols = pl.ds(start, wide)
            d_out[rows_of(0), cols] = jnp.where(is_x, d_gate, 0.0).astype(BF16)
            d_out[rows_of(1), cols] = jnp.where(is_x, d_up, 0.0).astype(BF16)
            d_out[rows_of(2), cols] = jnp.where(is_x, 0.0, hid).astype(BF16)
            return carry

        lax.fori_loop(0, hidden // tall, pointwise, 0)
        return carry

    lax.fori_loop(0, total // wide, products, 0)

    d_rows[...] = lax.dot_general(
        select[...], d_out[pl.ds(0, 2 * hidden), :], NT, preferred_element_type=F32
    ).astype(BF16)
    narrow = 256

    def terms(i, carry):
        sides = []
        for h in range(2):
            cols = pl.ds(pl.multiple_of(h * half + i * narrow, narrow), narrow)
            term = jnp.dot(d_rows[...], w[pl.ds(0, 2 * hidden), cols], preferred_element_type=F32)
            sides.append(term.reshape(n_dp, kept, narrow))
        both = jnp.concatenate(sides, axis=1).astype(BF16)
        part[:, :, pl.ds(pl.multiple_of(i * narrow, narrow), narrow)] = both
        return carry

    lax.fori_loop(0, half // narrow, terms, 0)

    def pair(k_offset):
        k = chip_at(spot + k_offset)
        return pltpu.make_async_remote_copy(
            src_ref=part.at[(1 - core) * chips + k], dst_ref=sib.at[k],
            send_sem=pair_send.at[k_offset], recv_sem=pair_recv.at[k_offset],
            device_id=sibling, device_id_type=MESH,
        )

    offsets = [far]
    for step in range(far - 1, 0, -1):
        offsets += [step, chips - step]
    offsets.append(0)
    pairs = {}
    for offset in offsets:
        pairs[offset] = pair(offset)
        pairs[offset].start()

    def rs(way, step, h):
        cols = pl.ds(h * quarter, quarter)
        return pltpu.make_async_remote_copy(
            src_ref=out_buf.at[way, step, :, cols], dst_ref=in_buf.at[way, step, :, cols],
            send_sem=rs_send.at[way, step, h], recv_sem=rs_recv.at[way, step, h],
            device_id=neighbour[way], device_id_type=MESH,
        )

    def begins(way, step, h):
        return step > 0 or way == h

    ready = set()
    sums = []
    for step in range(far):
        distance = far - step
        for h in range(2):
            cols = pl.ds(h * quarter, quarter)
            for way in range(2):
                if not begins(way, step, h):
                    continue
                offset = distance if way == 0 else chips - distance
                if offset not in ready:
                    pairs[offset].wait_recv()
                    ready.add(offset)
                k = chip_at(spot + offset)
                value = part[core * chips + k, :, cols].astype(F32) + sib[k, :, cols].astype(F32)
                if step > 0 and begins(way, step - 1, h):
                    rs(way, step - 1, h).wait_recv()
                    value += in_buf[way, step - 1, :, cols].astype(F32)
                out_buf[way, step, :, cols] = value.astype(BF16)
                rs(way, step, h).start()
                sums.append((way, step, h))
    pairs[0].wait_recv()
    own = part[core * chips + chip].astype(F32) + sib[chip].astype(F32)
    for way in range(2):
        for h in range(2):
            rs(way, far - 1, h).wait_recv()
        own += in_buf[way, far - 1].astype(F32)
    back_out[mine] = own.astype(BF16)

    returns = []
    for step in range(1, window):
        other = lax.rem(mine + step, window)
        returns.append(pltpu.make_async_remote_copy(
            src_ref=back_out.at[mine], dst_ref=back_out.at[mine],
            send_sem=z_send.at[step], recv_sem=z_recv.at[step],
            device_id=(me, other), device_id_type=MESH,
        ))
        returns[-1].start()
    for copy in swaps + hops + shares:
        copy.wait_send()
    for copy in pairs.values():
        copy.wait_send()
    for key in sums:
        rs(*key).wait_send()
    for copy in returns:
        copy.wait()
    gathered.wait()


def gradient_kernel(hidden, rows, d, back, pick, token_grad, grad_gate, grad_up, grad_down):
    for index, out in enumerate((grad_gate, grad_up, grad_down)):
        out[...] = jnp.dot(
            d[pl.ds(index * hidden, hidden), :], rows[...], preferred_element_type=F32
        ).astype(out.dtype)
    token_grad[...] = jnp.dot(pick[0], back[...], preferred_element_type=F32).astype(token_grad.dtype)


def selection(n_dp, window):
    chips, kept, group = n_dp // 2, window * CAP, 2 * CAP
    table = np.zeros((n_dp * kept, n_dp * window * group), np.float32)
    for core in range(2):
        for chip in range(chips):
            for row in range(kept):
                source, slot = divmod(row, CAP)
                column = (2 * chip + core) * window * group + source * group + slot
                table[(core * chips + chip) * kept + row, column] = 1.0
    return table


def shards(n_dp, window, tokens, cotangent, experts, route_weight, w_gate, w_up, w_down):
    count, width = tokens.shape
    hidden = w_gate.shape[1]
    half = width // 2
    chips = n_dp // 2
    far = chips // 2
    kept = window * CAP
    block = 2 * kept
    total = n_dp * block
    wide = 256 if total % 256 == 0 else total
    vmem = pl.BlockSpec(memory_space=pltpu.VMEM)
    anywhere = pl.BlockSpec(memory_space=pl.ANY)
    dma = pltpu.SemaphoreType.DMA
    flops = 2 * hidden * width * total
    rows, d, back, pick = pl.pallas_call(
        functools.partial(exchange_kernel, n_dp, window),
        out_shape=(
            jax.ShapeDtypeStruct((n_dp, block, width), BF16),
            jax.ShapeDtypeStruct((3 * hidden, total), BF16),
            jax.ShapeDtypeStruct((window, block, half), BF16),
            jax.ShapeDtypeStruct((2, count, window * block), BF16),
        ),
        in_specs=[vmem] * 5 + [anywhere] * 3,
        out_specs=(anywhere, vmem, vmem, vmem),
        scratch_shapes=[
            pltpu.VMEM((3 * hidden, width), BF16),
            pltpu.VMEM((window, 4 * CAP, half), BF16),
            pltpu.VMEM((window, 4 * CAP, half), BF16),
            pltpu.VMEM((n_dp, block, width), BF16),
            pltpu.VMEM((3 * hidden, wide), F32),
            pltpu.VMEM((n_dp * kept, 2 * hidden), BF16),
            pltpu.VMEM((n_dp, block, half), BF16),
            pltpu.VMEM((chips, block, half), BF16),
            pltpu.VMEM((2, far, block, half), BF16),
            pltpu.VMEM((2, far, block, half), BF16),
            dma((3,)),
            dma((window,)),
            dma((window,)),
            dma((2, far, 2)),
            dma((2, far, 2)),
            dma((2, far + 1, 2)),
            dma((2, far + 1, 2)),
            dma((chips,)),
            dma((chips,)),
            dma((2, far, 2)),
            dma((2, far, 2)),
            dma((window,)),
            dma((window,)),
            dma,
        ],
        compiler_params=pltpu.CompilerParams(
            collective_id=0, has_side_effects=True, vmem_limit_bytes=60 * 1024 * 1024
        ),
        cost_estimate=pl.CostEstimate(
            flops=5 * flops, bytes_accessed=2 * (3 * hidden + 2 * count + total) * width, transcendentals=0
        ),
        name="exchange",
    )(
        tokens, cotangent, experts, route_weight, jnp.asarray(selection(n_dp, window), BF16),
        w_gate[0], w_up[0], w_down[0],
    )

    step = half // 2
    grads = jax.ShapeDtypeStruct((hidden, width), BF16)
    token_grad, grad_g, grad_u, grad_d = pl.pallas_call(
        functools.partial(gradient_kernel, hidden),
        grid=(4,),
        out_shape=(jax.ShapeDtypeStruct((count, width), BF16), grads, grads, grads),
        in_specs=[
            pl.BlockSpec((total, step), lambda i: (0, i)),
            pl.BlockSpec((3 * hidden, total), lambda i: (0, 0)),
            pl.BlockSpec((window * block, step), lambda i: (0, lax.rem(i, 2))),
            pl.BlockSpec((1, count, window * block), lambda i: (lax.div(i, 2), 0, 0)),
        ],
        out_specs=(
            pl.BlockSpec((count, step), lambda i: (0, i)),
            *[pl.BlockSpec((hidden, step), lambda i: (0, i))] * 3,
        ),
        compiler_params=pltpu.CompilerParams(vmem_limit_bytes=60 * 1024 * 1024),
        cost_estimate=pl.CostEstimate(
            flops=3 * flops, bytes_accessed=2 * (3 * hidden + count + total) * width, transcendentals=0
        ),
        name="gradients",
    )(rows.reshape(total, width), d, back.reshape(window * block, half), pick)
    return token_grad, grad_g[None], grad_u[None], grad_d[None]


def solution(mesh):
    by_token = P(("dp", "expert"), None)
    by_expert = P("expert", "dp", None)
    return jax.shard_map(
        functools.partial(shards, mesh.shape["dp"], mesh.shape["expert"]),
        mesh=mesh,
        in_specs=(by_token,) * 4 + (by_expert,) * 3,
        out_specs=(by_token,) + (by_expert,) * 3,
        check_vma=False,
    )
```

time: 177 us -> 63 us (0.36)
  Pallas kernels: 0 us -> 59.2 us
  blocking collectives: 47.6 us -> 0 us
  waiting for transfers between devices: 44.2 us -> 0 us
  local copies, waits for them, and re-layouts: 27.9 us -> 2.83 us
  matrix products: 17 us -> 0 us
  other arithmetic: 14.5 us -> 0 us
  between operations: 14.2 us -> 0.64 us
  starting transfers between devices: 11 us -> 0 us
    pallas_call x0 -> x2, Pallas kernels: none -> 59.2 us  [the longest x1 52.4 us: shards(): pl.pallas_call(functools.partial(exchange_kernel, n_dp, window), out_shap...]
    all_gather x2 -> x0, blocking collectives: 47.6 us -> none  [the longest x1 26.2 us: shards(): lax.all_gather(arrived[1], 'dp', axis=0, tiled=True)]
    reduce_scatter x1 -> x0, waiting for transfers between devices: 42.7 us -> none  [shards(): lax.psum_scatter(terms.astype(jnp.bfloat16), 'dp', scatter_dimension=0, t...]
    dot_general x8 -> x0, matrix products: 17 us -> none  [the longest x1 3.93 us: weight_terms(): jnp.einsum('rf,rd->fd', d_up, x_rows, preferred_element_type=jnp.float32)]
    all_to_all x3 -> x0, starting transfers between devices: 11 us -> none  [the longest x1 4.23 us: shards(): lax.all_to_all(c_slots, 'expert', split_axis=0, concat_axis=0, tiled=True)]
    reduce_sum x3 -> x0, other arithmetic: 8.95 us -> none  [the longest x1 8.78 us: shards(): token_grad = picked.reshape(-1, top, width).sum(axis=1).astype(jnp.bfloat16)]
    gather x5 -> x0, local copies, waits for them, and re-layouts: 7.63 us -> none  [the longest x1 3.09 us: shards(): returned[index].astype(jnp.float32)]
    reshape x5 -> x0, local copies, waits for them, and re-layouts: 6.37 us -> none  [the longest x1 2.38 us: shards(): c_rows = c_whole.reshape(-1, width)]
  transfers between devices with their start and end apart: 4 -> 0, of which waited for: 2 -> 0; matrix products, arithmetic and copies ran while one was open for 13% -> 0% of each run, Pallas kernels for 0% -> 0%
where the time goes in v1:
time: 63 us; the launch traced here: 62.7 us
  Pallas kernels  59.2 us (94%)
  local copies, waits for them, and re-layouts  2.83 us (4%)
  between operations  0.64 us (1%)
    pallas_call x1, Pallas kernels, shards(): pl.pallas_call(functools.partial(exchange_kernel, n_dp, window), out_shap...  52.4 us
    pallas_call x1, Pallas kernels, shards(): pl.pallas_call(functools.partial(gradient_kernel, hidden), grid=(4,), out...  6.86 us
    unnamed x2, local copies, waits for them, and re-layouts  2.83 us

profile of v1, /device:TPU:0, one launch (start us, length us, event | category | flops | bytes accessed | tf_op | source)
XLA Modules:
  0.0 62.7 jit_solution(15802729652785627852)
XLA Ops:
  0.6 1.4 %copy.12.experts = s32[128,2]{1,0:T(8,128)} copy(s32[128,2]{0,1:T(2,128)} %param.10) | data formatting | bytes 2048 | tf_op args[2]
  2.0 1.4 %copy.13.weights = f32[128,2]{1,0:T(8,128)} copy(f32[128,2]{0,1:T(2,128)} %param.11) | data formatting | bytes 2048 | tf_op args[3]
  3.5 52.4 %exchange.1 = (bf16[16,16,3584]{2,1,0:T(8,128)(2,1)}, bf16[1344,256]{1,0:T(8,128)(2,1)}, bf16[2,16,1792]{2,1,0:T(8,128)(2,1)}, bf16[2,128,32]{2,1,0:T(8,128)(2,1)}) custom-call(bf16[128,3584]{1,0:T(8,128)(2,1)} %tokens.1, bf16[128,3584]{1,0:T(8,128)(2,1)} %cotangent.1, s32[128,2]{1,0:T(8,128)} %copy.12.experts, f32[128,2]{1,0:T(8,128)} %copy.13.weights, ...), custom_call_target="tpu_custom_call" | custom-call | flops 4110417920 | bytes 13303808 | tf_op jit(solution)/shard_map/exchange/pallas_call | solution.py:344
  55.9 6.9 %gradients.1 = (bf16[128,3584]{1,0:T(8,128)(2,1)}, bf16[448,3584]{1,0:T(8,128)(2,1)}, bf16[448,3584]{1,0:T(8,128)(2,1)}, bf16[448,3584]{1,0:T(8,128)(2,1)}) custom-call(bf16[256,3584]{1,0:T(8,128)(2,1)} %bitcast.14, bf16[1344,256]{1,0:T(8,128)(2,1)} %get-tuple-element.13.d, bf16[32,1792]{1,0:T(8,128)(2,1)} %bitcast.15, ...), custom_call_target="tpu_custom_call" | custom-call | flops 2466250752 | bytes 12386304 | tf_op jit(solution)/shard_map/gradients/pallas_call | solution.py:394

commit v2 on v1

v2 whole, which is shorter than its diff:
```python
import functools

import jax
import jax.numpy as jnp
from jax import lax
from jax.experimental import pallas as pl
from jax.experimental.pallas import tpu as pltpu
from jax.sharding import PartitionSpec as P

CAP = 4
MESH = pl.DeviceIdType.MESH
F32 = jnp.float32
BF16 = jnp.bfloat16
NT = (((1,), (1,)), ((), ()))


def one_hots(experts, place_expert, place_slot):
    count = experts.shape[1]
    first = experts[0:1, :] == place_expert
    second = experts[1:2, :] == place_expert
    named = jnp.where(first | second, 1.0, 0.0).astype(F32)
    shape = (count, count)
    earlier = lax.broadcasted_iota(jnp.int32, shape, 0) < lax.broadcasted_iota(jnp.int32, shape, 1)
    earlier = jnp.where(earlier, 1.0, 0.0).astype(BF16)
    before = jnp.dot(named.astype(BF16), earlier, preferred_element_type=F32)
    return jnp.where(before == place_slot.astype(F32), named, 0.0), first


def exchange_kernel(
    n_dp, window,
    tokens, cotangent, experts, weights, w_gate, w_up, w_down,
    rows_out, d_out, back_out, pick_out,
    w, sent, arrived, rows, prod, d_rows, part, sib, out_buf, in_buf,
    w_sem, y_send, y_recv, ring_send, ring_recv, sib_send, sib_recv,
    pair_send, pair_recv, rs_send, rs_recv, z_send, z_recv, local_sem,
):
    width = tokens.shape[1]
    half = width // 2
    quarter = half // 2
    hidden = w_gate.shape[0]
    chips = n_dp // 2
    far = chips // 2
    group = 2 * CAP
    kept = window * CAP
    block = window * group
    total = n_dp * block

    me = lax.axis_index("dp")
    mine = lax.axis_index("expert")
    core = lax.rem(me, 2)
    chip = lax.div(me, 2)
    spot = jnp.where(lax.rem(chip, 2) == 0, lax.div(chip, 2), chips - 1 - lax.div(chip, 2))

    def chip_at(place):
        place = lax.rem(place + 2 * chips, chips)
        return jnp.where(place < far, 2 * place, 2 * (chips - 1 - place) + 1)

    def at(place):
        return 2 * chip_at(place) + core

    sibling = (2 * chip + 1 - core, mine)
    neighbour = ((at(spot + 1), mine), (at(spot - 1), mine))

    loads = []
    for index, source in enumerate((w_gate, w_up, w_down)):
        loads.append(pltpu.make_async_copy(source, w.at[pl.ds(index * hidden, hidden), :], w_sem.at[index]))
        loads[-1].start()

    barrier = pltpu.get_barrier_semaphore()
    greet = [sibling, *neighbour]
    for step in range(1, window):
        greet.append((me, lax.rem(mine + step, window)))
    for device in greet:
        pl.semaphore_signal(barrier, inc=1, device_id=device, device_id_type=MESH)

    place = lax.broadcasted_iota(jnp.int32, (block, 1), 0)
    match, first = one_hots(experts[...], lax.div(place, group), lax.rem(place, CAP))
    scale = jnp.where(first, weights[0:1, :], weights[1:2, :]) * match
    scale = jnp.sum(scale, axis=1, keepdims=True)
    is_x = lax.rem(lax.broadcasted_iota(jnp.int32, match.shape, 0), group) < CAP
    slots = jnp.dot(jnp.where(is_x, match, 0.0).astype(BF16), tokens[...], preferred_element_type=F32)
    slots += scale * jnp.dot(
        jnp.where(is_x, 0.0, match).astype(BF16), cotangent[...], preferred_element_type=F32
    )
    for e in range(window):
        piece = slots[e * group:(e + 1) * group]
        sent[e] = jnp.concatenate([piece[:, :half], piece[:, half:]], axis=0).astype(BF16)

    pl.semaphore_wait(barrier, len(greet))

    swaps = []
    for step in range(1, window):
        other = lax.rem(mine + step, window)
        swaps.append(pltpu.make_async_remote_copy(
            src_ref=sent.at[other], dst_ref=arrived.at[mine],
            send_sem=y_send.at[step], recv_sem=y_recv.at[step],
            device_id=(me, other), device_id_type=MESH,
        ))
        swaps[-1].start()
    arrived[mine] = sent[mine]

    columns = window * 2 * kept
    place = lax.broadcasted_iota(jnp.int32, (columns, 1), 0)
    row = lax.rem(place, kept)
    match, _ = one_hots(experts[...], lax.div(place, 2 * kept), lax.rem(row, CAP))
    match = jnp.transpose(jnp.where(lax.div(row, CAP) == mine, match, 0.0))
    side = lax.rem(lax.div(lax.broadcasted_iota(jnp.int32, (1, columns), 1), kept), 2)
    for h in range(2):
        pick_out[h] = jnp.where(side == h, match, 0.0).astype(BF16)

    for copy in swaps:
        copy.wait_recv()
    for h in range(2):
        own = [arrived[s].astype(F32)[h * group:(h + 1) * group] for s in range(window)]
        rows[me, :, pl.ds(h * half, half)] = jnp.concatenate(own, axis=0).astype(BF16)

    def view(way, step, q):
        origin = at(spot - step) if way == 0 else at(spot + step)
        return rows.at[origin, :, pl.ds(q * quarter, quarter)]

    def hop(way, step, q):
        return pltpu.make_async_remote_copy(
            src_ref=view(way, step, q), dst_ref=view(way, step, q),
            send_sem=ring_send.at[way, step, q], recv_sem=ring_recv.at[way, step, q],
            device_id=neighbour[way], device_id_type=MESH,
        )

    def share(way, step, q):
        return pltpu.make_async_remote_copy(
            src_ref=view(way, step, q), dst_ref=view(way, step, q),
            send_sem=sib_send.at[way, step, q], recv_sem=sib_recv.at[way, step, q],
            device_id=sibling, device_id_type=MESH,
        )

    def travels(way, step, q):
        return step < far - 1 or (step == far - 1 and way == q % 2)

    hops, shares = [], [[], []]
    for q in range(4):
        for way in range(2):
            if travels(way, 0, q):
                hops.append(hop(way, 0, q))
                hops[-1].start()
    for q in range(4):
        shares[q // 2].append(share(0, 0, q))
        shares[q // 2][-1].start()
    for step in range(far):
        for q in range(4):
            for way in range(2):
                if travels(way, step, q):
                    hop(way, step, q).wait_recv()
                    if travels(way, step + 1, q):
                        hops.append(hop(way, step + 1, q))
                        hops[-1].start()
                    shares[q // 2].append(share(way, step + 1, q))
                    shares[q // 2][-1].start()
    for copy in loads:
        copy.wait()

    wide = 256 if total % 256 == 0 else total
    blocks = wide // block
    tall = 32
    x_lane = lax.rem(lax.broadcasted_iota(jnp.int32, (tall, wide), 1), group) < CAP

    def multiply(n, h):
        def matrix(index, carry):
            at_f = pl.ds(pl.multiple_of(index * hidden, hidden), hidden)
            at_k = pl.ds(h * half, half)
            piece = rows[pl.ds(n * blocks, blocks), :, at_k].reshape(wide, half)
            term = lax.dot_general(w[at_f, at_k], piece, NT, preferred_element_type=F32)
            prod[n, at_f, :] = term if h == 0 else prod[n, at_f, :] + term
            return carry

        lax.fori_loop(0, 3, matrix, 0)

    def first_half(n, carry):
        multiply(n, 0)
        return carry

    def products(n, carry):
        multiply(n, 1)
        start = pl.multiple_of(n * wide, wide)

        def pointwise(i, carry):
            def rows_of(index):
                return pl.ds(pl.multiple_of(index * hidden + i * tall, tall), tall)

            gate = prod[n, rows_of(0), :]
            up = prod[n, rows_of(1), :]
            back = pltpu.roll(prod[n, rows_of(2), :], wide - CAP, 1)
            sig = jax.nn.sigmoid(gate)
            act = gate * sig
            hid = pltpu.roll(act * up, CAP, 1)
            d_gate = back * up * sig * (1.0 + gate * (1.0 - sig))
            d_up = back * act
            cols = pl.ds(start, wide)
            d_out[rows_of(0), cols] = jnp.where(x_lane, d_gate, 0.0).astype(BF16)
            d_out[rows_of(1), cols] = jnp.where(x_lane, d_up, 0.0).astype(BF16)
            d_out[rows_of(2), cols] = jnp.where(x_lane, 0.0, hid).astype(BF16)
            return carry

        lax.fori_loop(0, hidden // tall, pointwise, 0)
        return carry

    for copy in shares[0]:
        copy.wait_recv()
    lax.fori_loop(0, total // wide, first_half, 0)
    for copy in shares[1]:
        copy.wait_recv()
    gathered = pltpu.make_async_copy(rows, rows_out, local_sem)
    gathered.start()
    lax.fori_loop(0, total // wide, products, 0)

    ordinal = lax.broadcasted_iota(jnp.int32, (n_dp * kept, 1), 0)
    owner = 2 * lax.rem(lax.div(ordinal, kept), chips) + lax.div(ordinal, kept * chips)
    slot = lax.rem(ordinal, kept)
    source = owner * block + lax.div(slot, CAP) * group + lax.rem(slot, CAP)
    select = lax.broadcasted_iota(jnp.int32, (n_dp * kept, total), 1) == source
    d_rows[...] = lax.dot_general(
        jnp.where(select, 1.0, 0.0).astype(BF16), d_out[pl.ds(0, 2 * hidden), :], NT, preferred_element_type=F32
    ).astype(BF16)
    narrow = 256
    chunks = half // narrow
    edges = (0, (chunks + 1) // 2 * narrow, half)

    def lanes_of(h):
        return pl.ds(edges[h], edges[h + 1] - edges[h])

    def terms(i, carry):
        sides = []
        for side in range(2):
            cols = pl.ds(pl.multiple_of(side * half + i * narrow, narrow), narrow)
            term = jnp.dot(d_rows[...], w[pl.ds(0, 2 * hidden), cols], preferred_element_type=F32)
            sides.append(term.reshape(n_dp, kept, narrow))
        both = jnp.concatenate(sides, axis=1).astype(BF16)
        part[:, :, pl.ds(pl.multiple_of(i * narrow, narrow), narrow)] = both
        return carry

    def pair(offset, h):
        k = chip_at(spot + offset)
        return pltpu.make_async_remote_copy(
            src_ref=part.at[(1 - core) * chips + k, :, lanes_of(h)], dst_ref=sib.at[k, :, lanes_of(h)],
            send_sem=pair_send.at[offset, h], recv_sem=pair_recv.at[offset, h],
            device_id=sibling, device_id_type=MESH,
        )

    offsets = [far]
    for step in range(far - 1, 0, -1):
        offsets += [step, chips - step]
    offsets.append(0)
    pairs = {}
    for h in range(2):
        lax.fori_loop(edges[h] // narrow, edges[h + 1] // narrow, terms, 0)
        for offset in offsets:
            pairs[offset, h] = pair(offset, h)
            pairs[offset, h].start()

    def rs(way, step, h):
        return pltpu.make_async_remote_copy(
            src_ref=out_buf.at[way, step, :, lanes_of(h)], dst_ref=in_buf.at[way, step, :, lanes_of(h)],
            send_sem=rs_send.at[way, step, h], recv_sem=rs_recv.at[way, step, h],
            device_id=neighbour[way], device_id_type=MESH,
        )

    def begins(way, step, h):
        return step > 0 or way == h

    ready = set()
    sums = []
    for step in range(far):
        distance = far - step
        for h in range(2):
            cols = lanes_of(h)
            for way in range(2):
                if not begins(way, step, h):
                    continue
                offset = distance if way == 0 else chips - distance
                if (offset, h) not in ready:
                    pairs[offset, h].wait_recv()
                    ready.add((offset, h))
                k = chip_at(spot + offset)
                value = part[core * chips + k, :, cols].astype(F32) + sib[k, :, cols].astype(F32)
                if step > 0 and begins(way, step - 1, h):
                    rs(way, step - 1, h).wait_recv()
                    value += in_buf[way, step - 1, :, cols].astype(F32)
                out_buf[way, step, :, cols] = value.astype(BF16)
                rs(way, step, h).start()
                sums.append((way, step, h))
    for h in range(2):
        pairs[0, h].wait_recv()
    own = part[core * chips + chip].astype(F32) + sib[chip].astype(F32)
    for way in range(2):
        for h in range(2):
            rs(way, far - 1, h).wait_recv()
        own += in_buf[way, far - 1].astype(F32)
    back_out[mine] = own.astype(BF16)

    returns = []
    for step in range(1, window):
        other = lax.rem(mine + step, window)
        returns.append(pltpu.make_async_remote_copy(
            src_ref=back_out.at[mine], dst_ref=back_out.at[mine],
            send_sem=z_send.at[step], recv_sem=z_recv.at[step],
            device_id=(me, other), device_id_type=MESH,
        ))
        returns[-1].start()
    for copy in swaps + hops + shares[0] + shares[1]:
        copy.wait_send()
    for copy in pairs.values():
        copy.wait_send()
    for key in sums:
        rs(*key).wait_send()
    for copy in returns:
        copy.wait()
    gathered.wait()


def gradient_kernel(hidden, rows, d, back, pick, token_grad, grad_gate, grad_up, grad_down):
    for index, out in enumerate((grad_gate, grad_up, grad_down)):
        out[...] = jnp.dot(
            d[pl.ds(index * hidden, hidden), :], rows[...], preferred_element_type=F32
        ).astype(out.dtype)
    token_grad[...] = jnp.dot(pick[0], back[...], preferred_element_type=F32).astype(token_grad.dtype)


def shards(n_dp, window, tokens, cotangent, experts, route_weight, w_gate, w_up, w_down):
    count, width = tokens.shape
    hidden = w_gate.shape[1]
    half = width // 2
    chips = n_dp // 2
    far = chips // 2
    kept = window * CAP
    block = 2 * kept
    total = n_dp * block
    wide = 256 if total % 256 == 0 else total
    vmem = pl.BlockSpec(memory_space=pltpu.VMEM)
    anywhere = pl.BlockSpec(memory_space=pl.ANY)
    dma = pltpu.SemaphoreType.DMA
    flops = 2 * hidden * width * total
    rows, d, back, pick = pl.pallas_call(
        functools.partial(exchange_kernel, n_dp, window),
        out_shape=(
            jax.ShapeDtypeStruct((n_dp, block, width), BF16),
            jax.ShapeDtypeStruct((3 * hidden, total), BF16),
            jax.ShapeDtypeStruct((window, block, half), BF16),
            jax.ShapeDtypeStruct((2, count, window * block), BF16),
        ),
        in_specs=[vmem] * 4 + [anywhere] * 3,
        out_specs=(anywhere, vmem, vmem, vmem),
        scratch_shapes=[
            pltpu.VMEM((3 * hidden, width), BF16),
            pltpu.VMEM((window, 4 * CAP, half), BF16),
            pltpu.VMEM((window, 4 * CAP, half), BF16),
            pltpu.VMEM((n_dp, block, width), BF16),
            pltpu.VMEM((total // wide, 3 * hidden, wide), F32),
            pltpu.VMEM((n_dp * kept, 2 * hidden), BF16),
            pltpu.VMEM((n_dp, block, half), BF16),
            pltpu.VMEM((chips, block, half), BF16),
            pltpu.VMEM((2, far, block, half), BF16),
            pltpu.VMEM((2, far, block, half), BF16),
            dma((3,)),
            dma((window,)),
            dma((window,)),
            dma((2, far, 4)),
            dma((2, far, 4)),
            dma((2, far + 1, 4)),
            dma((2, far + 1, 4)),
            dma((chips, 2)),
            dma((chips, 2)),
            dma((2, far, 2)),
            dma((2, far, 2)),
            dma((window,)),
            dma((window,)),
            dma,
        ],
        compiler_params=pltpu.CompilerParams(
            collective_id=0, has_side_effects=True, vmem_limit_bytes=60 * 1024 * 1024
        ),
        cost_estimate=pl.CostEstimate(
            flops=5 * flops, bytes_accessed=2 * (3 * hidden + 2 * count + total) * width, transcendentals=0
        ),
        name="exchange",
    )(
        tokens, cotangent, experts.T, route_weight.T,
        w_gate[0], w_up[0], w_down[0],
    )

    step = half // 2
    grads = jax.ShapeDtypeStruct((hidden, width), BF16)
    token_grad, grad_g, grad_u, grad_d = pl.pallas_call(
        functools.partial(gradient_kernel, hidden),
        grid=(4,),
        out_shape=(jax.ShapeDtypeStruct((count, width), BF16), grads, grads, grads),
        in_specs=[
            pl.BlockSpec((total, step), lambda i: (0, i)),
            pl.BlockSpec((3 * hidden, total), lambda i: (0, 0)),
            pl.BlockSpec((window * block, step), lambda i: (0, lax.rem(i, 2))),
            pl.BlockSpec((1, count, window * block), lambda i: (lax.div(i, 2), 0, 0)),
        ],
        out_specs=(
            pl.BlockSpec((count, step), lambda i: (0, i)),
            *[pl.BlockSpec((hidden, step), lambda i: (0, i))] * 3,
        ),
        compiler_params=pltpu.CompilerParams(vmem_limit_bytes=60 * 1024 * 1024),
        cost_estimate=pl.CostEstimate(
            flops=3 * flops, bytes_accessed=2 * (3 * hidden + count + total) * width, transcendentals=0
        ),
        name="gradients",
    )(rows.reshape(total, width), d, back.reshape(window * block, half), pick)
    return token_grad, grad_g[None], grad_u[None], grad_d[None]


def solution(mesh):
    by_token = P(("dp", "expert"), None)
    by_expert = P("expert", "dp", None)
    return jax.shard_map(
        functools.partial(shards, mesh.shape["dp"], mesh.shape["expert"]),
        mesh=mesh,
        in_specs=(by_token,) * 4 + (by_expert,) * 3,
        out_specs=(by_token,) + (by_expert,) * 3,
        check_vma=False,
    )
```

time: 63 us -> 57 us (0.905)
  Pallas kernels: 59.2 us -> 56.2 us
  local copies, waits for them, and re-layouts: 2.83 us -> 0 us
    pallas_call x1, Pallas kernels: 52.4 us -> 49.3 us  [shards(): pl.pallas_call(functools.partial(exchange_kernel, n_dp, window), out_shap...]
    unnamed x2 -> x0, local copies, waits for them, and re-layouts: 2.83 us -> none
where the time goes in v2:
time: 57 us; the launch traced here: 56.8 us
  Pallas kernels  56.2 us (99%)
  between operations  0.64 us (1%)
    pallas_call x1, Pallas kernels, shards(): pl.pallas_call(functools.partial(exchange_kernel, n_dp, window), out_shap...  49.3 us
    pallas_call x1, Pallas kernels, shards(): pl.pallas_call(functools.partial(gradient_kernel, hidden), grid=(4,), out...  6.86 us

profile of v2, /device:TPU:0, one launch (start us, length us, event | category | flops | bytes accessed | tf_op | source)
XLA Modules:
  0.0 56.8 jit_solution(9824098938944601021)
XLA Ops:
  0.6 49.3 %exchange.1 = (bf16[16,16,3584]{2,1,0:T(8,128)(2,1)}, bf16[1344,256]{1,0:T(8,128)(2,1)}, bf16[2,16,1792]{2,1,0:T(8,128)(2,1)}, bf16[2,128,32]{2,1,0:T(8,128)(2,1)}) custom-call(bf16[128,3584]{1,0:T(8,128)(2,1)} %tokens.1, bf16[128,3584]{1,0:T(8,128)(2,1)} %cotangent.1, s32[2,128]{1,0:T(2,128)} %bitcast.13, f32[2,128]{1,0:T(2,128)} %bitcast.14, ...), custom_call_target="tpu_custom_call" | custom-call | flops 4110417920 | bytes 13303808 | tf_op jit(solution)/shard_map/exchange/pallas_call | solution.py:340
  50.0 6.9 %gradients.1 = (bf16[128,3584]{1,0:T(8,128)(2,1)}, bf16[448,3584]{1,0:T(8,128)(2,1)}, bf16[448,3584]{1,0:T(8,128)(2,1)}, bf16[448,3584]{1,0:T(8,128)(2,1)}) custom-call(bf16[256,3584]{1,0:T(8,128)(2,1)} %bitcast.18, bf16[1344,256]{1,0:T(8,128)(2,1)} %get-tuple-element.13.d, bf16[32,1792]{1,0:T(8,128)(2,1)} %bitcast.19, ...), custom_call_target="tpu_custom_call" | custom-call | flops 2466250752 | bytes 12386304 | tf_op jit(solution)/shard_map/gradients/pallas_call | solution.py:390

commit v3 on v2

--- a/solution.py
+++ b/solution.py
@@ -29,10 +29,10 @@
 def exchange_kernel(
     n_dp, window,
     tokens, cotangent, experts, weights, w_gate, w_up, w_down,
-    rows_out, d_out, back_out, pick_out,
-    w, sent, arrived, rows, prod, d_rows, part, sib, out_buf, in_buf,
+    grads_out, back_out, pick_out,
+    returned, d_out, w, sent, arrived, rows, prod, d_rows, part, sib, out_buf, in_buf,
     w_sem, y_send, y_recv, ring_send, ring_recv, sib_send, sib_recv,
-    pair_send, pair_recv, rs_send, rs_recv, z_send, z_recv, local_sem,
+    pair_send, pair_recv, rs_send, rs_recv, z_send, z_recv,
 ):
     width = tokens.shape[1]
     half = width // 2
@@ -207,8 +207,6 @@
     lax.fori_loop(0, total // wide, first_half, 0)
     for copy in shares[1]:
         copy.wait_recv()
-    gathered = pltpu.make_async_copy(rows, rows_out, local_sem)
-    gathered.start()
     lax.fori_loop(0, total // wide, products, 0)
 
     ordinal = lax.broadcasted_iota(jnp.int32, (n_dp * kept, 1), 0)
@@ -264,6 +262,25 @@
 
     def begins(way, step, h):
         return step > 0 or way == h
+
+    strip = 512
+
+    def gradients(first, last):
+        def strip_of(i, carry):
+            cols = pl.ds(pl.multiple_of(i * strip, strip), strip)
+            piece = rows[:, :, cols].reshape(total, strip)
+
+            def matrix(index, carry):
+                at_f = pl.ds(pl.multiple_of(index * hidden, hidden), hidden)
+                grads_out[at_f, cols] = jnp.dot(d_out[at_f, :], piece, preferred_element_type=F32).astype(BF16)
+                return carry
+
+            return lax.fori_loop(0, 3, matrix, carry)
+
+        lax.fori_loop(first, last, strip_of, 0)
+
+    strips = width // strip
+    marks = [strips * 2 * step // (2 * far + 1) for step in range(far + 1)]
 
     ready = set()
     sums = []
@@ -286,6 +303,7 @@
                 out_buf[way, step, :, cols] = value.astype(BF16)
                 rs(way, step, h).start()
                 sums.append((way, step, h))
+        gradients(marks[step], marks[step + 1])
     for h in range(2):
         pairs[0, h].wait_recv()
     own = part[core * chips + chip].astype(F32) + sib[chip].astype(F32)
@@ -293,17 +311,18 @@
         for h in range(2):
             rs(way, far - 1, h).wait_recv()
         own += in_buf[way, far - 1].astype(F32)
-    back_out[mine] = own.astype(BF16)
+    returned[mine] = own.astype(BF16)
 
     returns = []
     for step in range(1, window):
         other = lax.rem(mine + step, window)
         returns.append(pltpu.make_async_remote_copy(
-            src_ref=back_out.at[mine], dst_ref=back_out.at[mine],
+            src_ref=returned.at[mine], dst_ref=returned.at[mine],
             send_sem=z_send.at[step], recv_sem=z_recv.at[step],
             device_id=(me, other), device_id_type=MESH,
         ))
         returns[-1].start()
+    gradients(marks[far], strips)
     for copy in swaps + hops + shares[0] + shares[1]:
         copy.wait_send()
     for copy in pairs.values():
@@ -312,15 +331,21 @@
         rs(*key).wait_send()
     for copy in returns:
         copy.wait()
-    gathered.wait()
-
-
-def gradient_kernel(hidden, rows, d, back, pick, token_grad, grad_gate, grad_up, grad_down):
+    back_out[...] = returned[...]
+
+
+def finish_kernel(hidden, grads, back, pick, token_grad, grad_gate, grad_up, grad_down, sem):
+    copies = []
     for index, out in enumerate((grad_gate, grad_up, grad_down)):
-        out[...] = jnp.dot(
-            d[pl.ds(index * hidden, hidden), :], rows[...], preferred_element_type=F32
-        ).astype(out.dtype)
-    token_grad[...] = jnp.dot(pick[0], back[...], preferred_element_type=F32).astype(token_grad.dtype)
+        copies.append(pltpu.make_async_copy(grads.at[pl.ds(index * hidden, hidden), :], out, sem.at[index]))
+        copies[-1].start()
+    window, block, half = back.shape
+    returned = back[...].reshape(window * block, half)
+    for h in range(2):
+        term = jnp.dot(pick[h], returned, preferred_element_type=F32)
+        token_grad[:, pl.ds(h * half, half)] = term.astype(token_grad.dtype)
+    for copy in copies:
+        copy.wait()
 
 
 def shards(n_dp, window, tokens, cotangent, experts, route_weight, w_gate, w_up, w_down):
@@ -337,17 +362,18 @@
     anywhere = pl.BlockSpec(memory_space=pl.ANY)
     dma = pltpu.SemaphoreType.DMA
     flops = 2 * hidden * width * total
-    rows, d, back, pick = pl.pallas_call(
+    grads, back, pick = pl.pallas_call(
         functools.partial(exchange_kernel, n_dp, window),
         out_shape=(
-            jax.ShapeDtypeStruct((n_dp, block, width), BF16),
-            jax.ShapeDtypeStruct((3 * hidden, total), BF16),
-            jax.ShapeDtypeStruct((window, block, half), BF16),
-            jax.ShapeDtypeStruct((2, count, window * block), BF16),
+            pltpu.VMEM((3 * hidden, width), BF16),
+            pltpu.VMEM((window, block, half), BF16),
+            pltpu.VMEM((2, count, window * block), BF16),
         ),
         in_specs=[vmem] * 4 + [anywhere] * 3,
-        out_specs=(anywhere, vmem, vmem, vmem),
+        out_specs=(vmem, vmem, vmem),
         scratch_shapes=[
+            pltpu.VMEM((window, block, half), BF16),
+            pltpu.VMEM((3 * hidden, total), BF16),
             pltpu.VMEM((3 * hidden, width), BF16),
             pltpu.VMEM((window, 4 * CAP, half), BF16),
             pltpu.VMEM((window, 4 * CAP, half), BF16),
@@ -371,10 +397,9 @@
             dma((2, far, 2)),
             dma((window,)),
             dma((window,)),
-            dma,
         ],
         compiler_params=pltpu.CompilerParams(
-            collective_id=0, has_side_effects=True, vmem_limit_bytes=60 * 1024 * 1024
+            collective_id=0, has_side_effects=True, vmem_limit_bytes=61 * 1024 * 1024 - 6 * hidden * width
         ),
         cost_estimate=pl.CostEstimate(
             flops=5 * flops, bytes_accessed=2 * (3 * hidden + 2 * count + total) * width, transcendentals=0
@@ -385,28 +410,20 @@
         w_gate[0], w_up[0], w_down[0],
     )
 
-    step = half // 2
-    grads = jax.ShapeDtypeStruct((hidden, width), BF16)
+    like = jax.ShapeDtypeStruct((hidden, width), BF16)
     token_grad, grad_g, grad_u, grad_d = pl.pallas_call(
-        functools.partial(gradient_kernel, hidden),
-        grid=(4,),
-        out_shape=(jax.ShapeDtypeStruct((count, width), BF16), grads, grads, grads),
-        in_specs=[
-            pl.BlockSpec((total, step), lambda i: (0, i)),
-            pl.BlockSpec((3 * hidden, total), lambda i: (0, 0)),
-            pl.BlockSpec((window * block, step), lambda i: (0, lax.rem(i, 2))),
-            pl.BlockSpec((1, count, window * block), lambda i: (lax.div(i, 2), 0, 0)),
-        ],
-        out_specs=(
-            pl.BlockSpec((count, step), lambda i: (0, i)),
-            *[pl.BlockSpec((hidden, step), lambda i: (0, i))] * 3,
+        functools.partial(finish_kernel, hidden),
+        out_shape=(jax.ShapeDtypeStruct((count, width), BF16), like, like, like),
+        in_specs=[vmem] * 3,
+        out_specs=(vmem, anywhere, anywhere, anywhere),
+        scratch_shapes=[dma((3,))],
+        compiler_params=pltpu.CompilerParams(vmem_limit_bytes=16 * 1024 * 1024),
+        cost_estimate=pl.CostEstimate(
+            flops=4 * count * window * block * half, bytes_accessed=2 * (3 * hidden + count) * width,
+            transcendentals=0,
         ),
-        compiler_params=pltpu.CompilerParams(vmem_limit_bytes=60 * 1024 * 1024),
-        cost_estimate=pl.CostEstimate(
-            flops=3 * flops, bytes_accessed=2 * (3 * hidden + count + total) * width, transcendentals=0
-        ),
-        name="gradients",
-    )(rows.reshape(total, width), d, back.reshape(window * block, half), pick)
+        name="finish",
+    )(*(pltpu.with_memory_space_constraint(array, pltpu.VMEM) for array in (grads, back, pick)))
     return token_grad, grad_g[None], grad_u[None], grad_d[None]
 
 

time: 57 us -> 53.7 us (0.942)
  Pallas kernels: 56.2 us -> 52.9 us
    pallas_call x1, Pallas kernels: 6.86 us -> 4.78 us  [shards(): pl.pallas_call(functools.partial(finish_kernel, hidden), out_shape=(jax.S...]
    pallas_call x1, Pallas kernels: 49.3 us -> 48.1 us  [shards(): pl.pallas_call(functools.partial(exchange_kernel, n_dp, window), out_shap...]
where the time goes in v3:
time: 53.7 us; the launch traced here: 53.5 us
  Pallas kernels  52.9 us (99%)
  between operations  0.64 us (1%)
    pallas_call x1, Pallas kernels, shards(): pl.pallas_call(functools.partial(exchange_kernel, n_dp, window), out_shap...  48.1 us
    pallas_call x1, Pallas kernels, shards(): pl.pallas_call(functools.partial(finish_kernel, hidden), out_shape=(jax.S...  4.78 us

profile of v3, /device:TPU:0, one launch (start us, length us, event | category | flops | bytes accessed | tf_op | source)
XLA Modules:
  0.0 53.5 jit_solution(12978912614821788088)
XLA Ops:
  0.6 48.1 %exchange.1 = (bf16[1344,3584]{1,0:T(8,128)(2,1)S(1)}, bf16[2,16,1792]{2,1,0:T(8,128)(2,1)S(1)}, bf16[2,128,32]{2,1,0:T(8,128)(2,1)S(1)}) custom-call(bf16[128,3584]{1,0:T(8,128)(2,1)} %tokens.1, bf16[128,3584]{1,0:T(8,128)(2,1)} %cotangent.1, s32[2,128]{1,0:T(2,128)} %bitcast.14, f32[2,128]{1,0:T(2,128)} %bitcast.15, bf16[448,3584]{1,0:T(8,128)(2,1)} %bitcast.8, ...), custom_call_target="tpu_custom_call" | custom-call | flops 4110417920 | bytes 13303808 | tf_op jit(solution)/shard_map/exchange/pallas_call | solution.py:365
  48.8 4.8 %finish.1 = (bf16[128,3584]{1,0:T(8,128)(2,1)}, bf16[448,3584]{1,0:T(8,128)(2,1)}, bf16[448,3584]{1,0:T(8,128)(2,1)}, bf16[448,3584]{1,0:T(8,128)(2,1)}) custom-call(bf16[1344,3584]{1,0:T(8,128)(2,1)S(1)} %get-tuple-element.11.grads, bf16[2,16,1792]{2,1,0:T(8,128)(2,1)S(1)} %get-tuple-element.12.back, bf16[2,128,32]{2,1,0:T(8,128)(2,1)S(1)} %get-tuple-element.13.pick), custom_call_target="tpu_custom_call" | custom-call | flops 29360128 | bytes 10551296 | tf_op jit(solution)/shard_map/finish/pallas_call | solution.py:414

commit v4 on v3

--- a/solution.py
+++ b/solution.py
@@ -28,13 +28,13 @@
 
 def exchange_kernel(
     n_dp, window,
-    tokens, cotangent, experts, weights, w_gate, w_up, w_down,
+    tokens_in, cotangent_in, experts, weights, w_gate, w_up, w_down,
     grads_out, back_out, pick_out,
-    returned, d_out, w, sent, arrived, rows, prod, d_rows, part, sib, out_buf, in_buf,
-    w_sem, y_send, y_recv, ring_send, ring_recv, sib_send, sib_recv,
+    tokens, cotangent, returned, d_out, w, sent, arrived, rows, prod, d_rows, part, sib, out_buf, in_buf,
+    in_sem, w_sem, y_send, y_recv, ring_send, ring_recv, sib_send, sib_recv,
     pair_send, pair_recv, rs_send, rs_recv, z_send, z_recv,
 ):
-    width = tokens.shape[1]
+    width = tokens_in.shape[1]
     half = width // 2
     quarter = half // 2
     hidden = w_gate.shape[0]
@@ -61,10 +61,15 @@
     sibling = (2 * chip + 1 - core, mine)
     neighbour = ((at(spot + 1), mine), (at(spot - 1), mine))
 
-    loads = []
-    for index, source in enumerate((w_gate, w_up, w_down)):
-        loads.append(pltpu.make_async_copy(source, w.at[pl.ds(index * hidden, hidden), :], w_sem.at[index]))
-        loads[-1].start()
+    inputs = []
+    for p in range(2):
+        cols = pl.ds(p * half, half)
+        inputs.append([
+            pltpu.make_async_copy(tokens_in.at[:, cols], tokens.at[:, cols], in_sem.at[0, p]),
+            pltpu.make_async_copy(cotangent_in.at[:, cols], cotangent.at[:, cols], in_sem.at[1, p]),
+        ])
+        for copy in inputs[-1]:
+            copy.start()
 
     barrier = pltpu.get_barrier_semaphore()
     greet = [sibling, *neighbour]
@@ -78,26 +83,75 @@
     scale = jnp.where(first, weights[0:1, :], weights[1:2, :]) * match
     scale = jnp.sum(scale, axis=1, keepdims=True)
     is_x = lax.rem(lax.broadcasted_iota(jnp.int32, match.shape, 0), group) < CAP
-    slots = jnp.dot(jnp.where(is_x, match, 0.0).astype(BF16), tokens[...], preferred_element_type=F32)
-    slots += scale * jnp.dot(
-        jnp.where(is_x, 0.0, match).astype(BF16), cotangent[...], preferred_element_type=F32
-    )
-    for e in range(window):
-        piece = slots[e * group:(e + 1) * group]
-        sent[e] = jnp.concatenate([piece[:, :half], piece[:, half:]], axis=0).astype(BF16)
-
-    pl.semaphore_wait(barrier, len(greet))
-
-    swaps = []
-    for step in range(1, window):
+    x_match = jnp.where(is_x, match, 0.0).astype(BF16)
+    c_match = jnp.where(is_x, 0.0, match).astype(BF16)
+
+    def swap(step, p):
         other = lax.rem(mine + step, window)
-        swaps.append(pltpu.make_async_remote_copy(
-            src_ref=sent.at[other], dst_ref=arrived.at[mine],
-            send_sem=y_send.at[step], recv_sem=y_recv.at[step],
+        lanes = pl.ds(p * quarter, quarter)
+        return pltpu.make_async_remote_copy(
+            src_ref=sent.at[other, :, lanes], dst_ref=arrived.at[mine, :, lanes],
+            send_sem=y_send.at[step, p], recv_sem=y_recv.at[step, p],
             device_id=(me, other), device_id_type=MESH,
-        ))
-        swaps[-1].start()
-    arrived[mine] = sent[mine]
+        )
+
+    swaps, loads = [], []
+    for p in range(2):
+        cols = pl.ds(p * half, half)
+        for copy in inputs[p]:
+            copy.wait()
+        slots = jnp.dot(x_match, tokens[:, cols], preferred_element_type=F32)
+        slots += scale * jnp.dot(c_match, cotangent[:, cols], preferred_element_type=F32)
+        lanes = pl.ds(p * quarter, quarter)
+        for e in range(window):
+            piece = slots[e * group:(e + 1) * group]
+            sent[e, :, lanes] = jnp.concatenate([piece[:, :quarter], piece[:, quarter:]], axis=0).astype(BF16)
+        if p == 0:
+            pl.semaphore_wait(barrier, len(greet))
+        swaps.append([swap(step, p) for step in range(1, window)])
+        for copy in swaps[p]:
+            copy.start()
+        arrived[mine, :, lanes] = sent[mine, :, lanes]
+    for index, source in enumerate((w_gate, w_up, w_down)):
+        loads.append(pltpu.make_async_copy(source, w.at[pl.ds(index * hidden, hidden), :], w_sem.at[index]))
+        loads[-1].start()
+
+    def view(way, step, q):
+        origin = at(spot - step) if way == 0 else at(spot + step)
+        return rows.at[origin, :, pl.ds(q * quarter, quarter)]
+
+    def hop(way, step, q):
+        return pltpu.make_async_remote_copy(
+            src_ref=view(way, step, q), dst_ref=view(way, step, q),
+            send_sem=ring_send.at[way, step, q], recv_sem=ring_recv.at[way, step, q],
+            device_id=neighbour[way], device_id_type=MESH,
+        )
+
+    def share(way, step, q):
+        return pltpu.make_async_remote_copy(
+            src_ref=view(way, step, q), dst_ref=view(way, step, q),
+            send_sem=sib_send.at[way, step, q], recv_sem=sib_recv.at[way, step, q],
+            device_id=sibling, device_id_type=MESH,
+        )
+
+    def travels(way, step, q):
+        return step < far - 1 or (step == far - 1 and way == q % 2)
+
+    hops, shares = [], [[], []]
+    for p in range(2):
+        for copy in swaps[p]:
+            copy.wait_recv()
+        for q in (2 * p, 2 * p + 1):
+            side = (q % 2) * group
+            lanes = pl.ds(p * quarter, quarter)
+            own = [arrived[s, :, lanes].astype(F32)[side:side + group] for s in range(window)]
+            rows[me, :, pl.ds(q * quarter, quarter)] = jnp.concatenate(own, axis=0).astype(BF16)
+            for way in range(2):
+                if travels(way, 0, q):
+                    hops.append(hop(way, 0, q))
+                    hops[-1].start()
+            shares[p].append(share(0, 0, q))
+            shares[p][-1].start()
 
     columns = window * 2 * kept
     place = lax.broadcasted_iota(jnp.int32, (columns, 1), 0)
@@ -108,42 +162,6 @@
     for h in range(2):
         pick_out[h] = jnp.where(side == h, match, 0.0).astype(BF16)
 
-    for copy in swaps:
-        copy.wait_recv()
-    for h in range(2):
-        own = [arrived[s].astype(F32)[h * group:(h + 1) * group] for s in range(window)]
-        rows[me, :, pl.ds(h * half, half)] = jnp.concatenate(own, axis=0).astype(BF16)
-
-    def view(way, step, q):
-        origin = at(spot - step) if way == 0 else at(spot + step)
-        return rows.at[origin, :, pl.ds(q * quarter, quarter)]
-
-    def hop(way, step, q):
-        return pltpu.make_async_remote_copy(
-            src_ref=view(way, step, q), dst_ref=view(way, step, q),
-            send_sem=ring_send.at[way, step, q], recv_sem=ring_recv.at[way, step, q],
-            device_id=neighbour[way], device_id_type=MESH,
-        )
-
-    def share(way, step, q):
-        return pltpu.make_async_remote_copy(
-            src_ref=view(way, step, q), dst_ref=view(way, step, q),
-            send_sem=sib_send.at[way, step, q], recv_sem=sib_recv.at[way, step, q],
-            device_id=sibling, device_id_type=MESH,
-        )
-
-    def travels(way, step, q):
-        return step < far - 1 or (step == far - 1 and way == q % 2)
-
-    hops, shares = [], [[], []]
-    for q in range(4):
-        for way in range(2):
-            if travels(way, 0, q):
-                hops.append(hop(way, 0, q))
-                hops[-1].start()
-    for q in range(4):
-        shares[q // 2].append(share(0, 0, q))
-        shares[q // 2][-1].start()
     for step in range(far):
         for q in range(4):
             for way in range(2):
@@ -159,7 +177,7 @@
 
     wide = 256 if total % 256 == 0 else total
     blocks = wide // block
-    tall = 32
+    tall = 112 if hidden % 112 == 0 else 16
     x_lane = lax.rem(lax.broadcasted_iota(jnp.int32, (tall, wide), 1), group) < CAP
 
     def multiply(n, h):
@@ -304,26 +322,25 @@
                 rs(way, step, h).start()
                 sums.append((way, step, h))
         gradients(marks[step], marks[step + 1])
+    returns = []
     for h in range(2):
+        cols = lanes_of(h)
         pairs[0, h].wait_recv()
-    own = part[core * chips + chip].astype(F32) + sib[chip].astype(F32)
-    for way in range(2):
-        for h in range(2):
+        own = part[core * chips + chip, :, cols].astype(F32) + sib[chip, :, cols].astype(F32)
+        for way in range(2):
             rs(way, far - 1, h).wait_recv()
-        own += in_buf[way, far - 1].astype(F32)
-    returned[mine] = own.astype(BF16)
-
-    returns = []
-    for step in range(1, window):
-        other = lax.rem(mine + step, window)
-        returns.append(pltpu.make_async_remote_copy(
-            src_ref=returned.at[mine], dst_ref=returned.at[mine],
-            send_sem=z_send.at[step], recv_sem=z_recv.at[step],
-            device_id=(me, other), device_id_type=MESH,
-        ))
-        returns[-1].start()
+            own += in_buf[way, far - 1, :, cols].astype(F32)
+        returned[mine, :, cols] = own.astype(BF16)
+        for step in range(1, window):
+            other = lax.rem(mine + step, window)
+            returns.append(pltpu.make_async_remote_copy(
+                src_ref=returned.at[mine, :, cols], dst_ref=returned.at[mine, :, cols],
+                send_sem=z_send.at[step, h], recv_sem=z_recv.at[step, h],
+                device_id=(me, other), device_id_type=MESH,
+            ))
+            returns[-1].start()
     gradients(marks[far], strips)
-    for copy in swaps + hops + shares[0] + shares[1]:
+    for copy in swaps[0] + swaps[1] + hops + shares[0] + shares[1]:
         copy.wait_send()
     for copy in pairs.values():
         copy.wait_send()
@@ -334,16 +351,25 @@
     back_out[...] = returned[...]
 
 
-def finish_kernel(hidden, grads, back, pick, token_grad, grad_gate, grad_up, grad_down, sem):
+def finish_kernel(hidden, grads, back, pick, token_grad, grad_gate, grad_up, grad_down, summed, sem):
     copies = []
+    pieces = sem.shape[1]
+    tall = hidden // pieces
     for index, out in enumerate((grad_gate, grad_up, grad_down)):
-        copies.append(pltpu.make_async_copy(grads.at[pl.ds(index * hidden, hidden), :], out, sem.at[index]))
-        copies[-1].start()
+        for piece in range(pieces):
+            copies.append(pltpu.make_async_copy(
+                grads.at[pl.ds(index * hidden + piece * tall, tall), :],
+                out.at[pl.ds(piece * tall, tall), :], sem.at[index, piece],
+            ))
+            copies[-1].start()
     window, block, half = back.shape
     returned = back[...].reshape(window * block, half)
     for h in range(2):
         term = jnp.dot(pick[h], returned, preferred_element_type=F32)
-        token_grad[:, pl.ds(h * half, half)] = term.astype(token_grad.dtype)
+        cols = pl.ds(h * half, half)
+        summed[:, cols] = term.astype(BF16)
+        copies.append(pltpu.make_async_copy(summed.at[:, cols], token_grad.at[:, cols], sem.at[3, h]))
+        copies[-1].start()
     for copy in copies:
         copy.wait()
 
@@ -369,9 +395,11 @@
             pltpu.VMEM((window, block, half), BF16),
             pltpu.VMEM((2, count, window * block), BF16),
         ),
-        in_specs=[vmem] * 4 + [anywhere] * 3,
+        in_specs=[anywhere] * 2 + [vmem] * 2 + [anywhere] * 3,
         out_specs=(vmem, vmem, vmem),
         scratch_shapes=[
+            pltpu.VMEM((count, width), BF16),
+            pltpu.VMEM((count, width), BF16),
             pltpu.VMEM((window, block, half), BF16),
             pltpu.VMEM((3 * hidden, total), BF16),
             pltpu.VMEM((3 * hidden, width), BF16),
@@ -384,9 +412,10 @@
             pltpu.VMEM((chips, block, half), BF16),
             pltpu.VMEM((2, far, block, half), BF16),
             pltpu.VMEM((2, far, block, half), BF16),
+            dma((2, 2)),
             dma((3,)),
-            dma((window,)),
-            dma((window,)),
+            dma((window, 2)),
+            dma((window, 2)),
             dma((2, far, 4)),
             dma((2, far, 4)),
             dma((2, far + 1, 4)),
@@ -395,8 +424,8 @@
             dma((chips, 2)),
             dma((2, far, 2)),
             dma((2, far, 2)),
-            dma((window,)),
-            dma((window,)),
+            dma((window, 2)),
+            dma((window, 2)),
         ],
         compiler_params=pltpu.CompilerParams(
             collective_id=0, has_side_effects=True, vmem_limit_bytes=61 * 1024 * 1024 - 6 * hidden * width
@@ -415,8 +444,8 @@
         functools.partial(finish_kernel, hidden),
         out_shape=(jax.ShapeDtypeStruct((count, width), BF16), like, like, like),
         in_specs=[vmem] * 3,
-        out_specs=(vmem, anywhere, anywhere, anywhere),
-        scratch_shapes=[dma((3,))],
+        out_specs=(anywhere,) * 4,
+        scratch_shapes=[pltpu.VMEM((count, width), BF16), dma((4, 7 if hidden % 112 == 0 else 2))],
         compiler_params=pltpu.CompilerParams(vmem_limit_bytes=16 * 1024 * 1024),
         cost_estimate=pl.CostEstimate(
             flops=4 * count * window * block * half, bytes_accessed=2 * (3 * hidden + count) * width,

time: 53.7 us -> 51.3 us (0.955)
  Pallas kernels: 52.9 us -> 50.5 us
    pallas_call x1, Pallas kernels: 48.1 us -> 46.4 us  [shards(): pl.pallas_call(functools.partial(exchange_kernel, n_dp, window), out_shap...]
    pallas_call x1, Pallas kernels: 4.78 us -> 4.18 us  [shards(): pl.pallas_call(functools.partial(finish_kernel, hidden), out_shape=(jax.S...]
where the time goes in v4:
time: 51.3 us; the launch traced here: 51.2 us
  Pallas kernels  50.5 us (98%)
  between operations  0.64 us (1%)
    pallas_call x1, Pallas kernels, shards(): pl.pallas_call(functools.partial(exchange_kernel, n_dp, window), out_shap...  46.4 us
    pallas_call x1, Pallas kernels, shards(): pl.pallas_call(functools.partial(finish_kernel, hidden), out_shape=(jax.S...  4.18 us

profile of v4, /device:TPU:0, one launch (start us, length us, event | category | flops | bytes accessed | tf_op | source)
XLA Modules:
  0.0 51.2 jit_solution(13693636710891028426)
XLA Ops:
  0.6 46.4 %exchange.1 = (bf16[1344,3584]{1,0:T(8,128)(2,1)S(1)}, bf16[2,16,1792]{2,1,0:T(8,128)(2,1)S(1)}, bf16[2,128,32]{2,1,0:T(8,128)(2,1)S(1)}) custom-call(bf16[128,3584]{1,0:T(8,128)(2,1)} %tokens_in.1, bf16[128,3584]{1,0:T(8,128)(2,1)} %cotangent_in.1, s32[2,128]{1,0:T(2,128)} %bitcast.14, f32[2,128]{1,0:T(2,128)} %bitcast.15, bf16[448,3584]{1,0:T(8,128)(2,1)} %bitcast.8, ...), custom_call_target="tpu_custom_call" | custom-call | flops 4110417920 | bytes 13303808 | tf_op jit(solution)/shard_map/exchange/pallas_call | solution.py:391
  47.0 4.2 %finish.1 = (bf16[128,3584]{1,0:T(8,128)(2,1)}, bf16[448,3584]{1,0:T(8,128)(2,1)}, bf16[448,3584]{1,0:T(8,128)(2,1)}, bf16[448,3584]{1,0:T(8,128)(2,1)}) custom-call(bf16[1344,3584]{1,0:T(8,128)(2,1)S(1)} %get-tuple-element.11.grads, bf16[2,16,1792]{2,1,0:T(8,128)(2,1)S(1)} %get-tuple-element.12.back, bf16[2,128,32]{2,1,0:T(8,128)(2,1)S(1)} %get-tuple-element.13.pick), custom_call_target="tpu_custom_call" | custom-call | flops 29360128 | bytes 10551296 | tf_op jit(solution)/shard_map/finish/pallas_call | solution.py:443

commit v5 on v4

--- a/solution.py
+++ b/solution.py
@@ -181,15 +181,10 @@
     x_lane = lax.rem(lax.broadcasted_iota(jnp.int32, (tall, wide), 1), group) < CAP
 
     def multiply(n, h):
-        def matrix(index, carry):
-            at_f = pl.ds(pl.multiple_of(index * hidden, hidden), hidden)
-            at_k = pl.ds(h * half, half)
-            piece = rows[pl.ds(n * blocks, blocks), :, at_k].reshape(wide, half)
-            term = lax.dot_general(w[at_f, at_k], piece, NT, preferred_element_type=F32)
-            prod[n, at_f, :] = term if h == 0 else prod[n, at_f, :] + term
-            return carry
-
-        lax.fori_loop(0, 3, matrix, 0)
+        at_k = pl.ds(h * half, half)
+        piece = rows[pl.ds(n * blocks, blocks), :, at_k].reshape(wide, half)
+        term = lax.dot_general(w[:, at_k], piece, NT, preferred_element_type=F32)
+        prod[n] = term if h == 0 else prod[n] + term
 
     def first_half(n, carry):
         multiply(n, 0)
@@ -281,24 +276,21 @@
     def begins(way, step, h):
         return step > 0 or way == h
 
-    strip = 512
-
-    def gradients(first, last):
-        def strip_of(i, carry):
-            cols = pl.ds(pl.multiple_of(i * strip, strip), strip)
-            piece = rows[:, :, cols].reshape(total, strip)
-
-            def matrix(index, carry):
-                at_f = pl.ds(pl.multiple_of(index * hidden, hidden), hidden)
-                grads_out[at_f, cols] = jnp.dot(d_out[at_f, :], piece, preferred_element_type=F32).astype(BF16)
-                return carry
-
-            return lax.fori_loop(0, 3, matrix, carry)
-
+    strip = 256
+    strips = width // strip
+    gaps = 2 * far + 3
+    done = 0
+
+    def strip_of(i, carry):
+        cols = pl.ds(pl.multiple_of(i * strip, strip), strip)
+        piece = rows[:, :, cols].reshape(total, strip)
+        grads_out[:, cols] = jnp.dot(d_out[...], piece, preferred_element_type=F32).astype(BF16)
+        return carry
+
+    def gradients(first, gap):
+        last = strips if gap == gaps else strips * gap // gaps
         lax.fori_loop(first, last, strip_of, 0)
-
-    strips = width // strip
-    marks = [strips * 2 * step // (2 * far + 1) for step in range(far + 1)]
+        return last
 
     ready = set()
     sums = []
@@ -321,7 +313,7 @@
                 out_buf[way, step, :, cols] = value.astype(BF16)
                 rs(way, step, h).start()
                 sums.append((way, step, h))
-        gradients(marks[step], marks[step + 1])
+            done = gradients(done, 2 * step + h + 1)
     returns = []
     for h in range(2):
         cols = lanes_of(h)
@@ -339,7 +331,7 @@
                 device_id=(me, other), device_id_type=MESH,
             ))
             returns[-1].start()
-    gradients(marks[far], strips)
+    gradients(done, gaps)
     for copy in swaps[0] + swaps[1] + hops + shares[0] + shares[1]:
         copy.wait_send()
     for copy in pairs.values():

time: 51.3 us -> 53.3 us (1.039)
  Pallas kernels: 50.5 us -> 52.5 us
    pallas_call x1, Pallas kernels: 46.4 us -> 48.3 us  [shards(): pl.pallas_call(functools.partial(exchange_kernel, n_dp, window), out_shap...]
where the time goes in v5:
time: 53.3 us; the launch traced here: 53.1 us
  Pallas kernels  52.5 us (98%)
  between operations  0.64 us (1%)
    pallas_call x1, Pallas kernels, shards(): pl.pallas_call(functools.partial(exchange_kernel, n_dp, window), out_shap...  48.3 us
    pallas_call x1, Pallas kernels, shards(): pl.pallas_call(functools.partial(finish_kernel, hidden), out_shape=(jax.S...  4.18 us

profile of v5, /device:TPU:0, one launch (start us, length us, event | category | flops | bytes accessed | tf_op | source)
XLA Modules:
  0.0 53.1 jit_solution(238449975571643073)
XLA Ops:
  0.6 48.3 %exchange.1 = (bf16[1344,3584]{1,0:T(8,128)(2,1)S(1)}, bf16[2,16,1792]{2,1,0:T(8,128)(2,1)S(1)}, bf16[2,128,32]{2,1,0:T(8,128)(2,1)S(1)}) custom-call(bf16[128,3584]{1,0:T(8,128)(2,1)} %tokens_in.1, bf16[128,3584]{1,0:T(8,128)(2,1)} %cotangent_in.1, s32[2,128]{1,0:T(2,128)} %bitcast.14, f32[2,128]{1,0:T(2,128)} %bitcast.15, bf16[448,3584]{1,0:T(8,128)(2,1)} %bitcast.8, ...), custom_call_target="tpu_custom_call" | custom-call | flops 4110417920 | bytes 13303808 | tf_op jit(solution)/shard_map/exchange/pallas_call | solution.py:383
  48.9 4.2 %finish.1 = (bf16[128,3584]{1,0:T(8,128)(2,1)}, bf16[448,3584]{1,0:T(8,128)(2,1)}, bf16[448,3584]{1,0:T(8,128)(2,1)}, bf16[448,3584]{1,0:T(8,128)(2,1)}) custom-call(bf16[1344,3584]{1,0:T(8,128)(2,1)S(1)} %get-tuple-element.11.grads, bf16[2,16,1792]{2,1,0:T(8,128)(2,1)S(1)} %get-tuple-element.12.back, bf16[2,128,32]{2,1,0:T(8,128)(2,1)S(1)} %get-tuple-element.13.pick), custom_call_target="tpu_custom_call" | custom-call | flops 29360128 | bytes 10551296 | tf_op jit(solution)/shard_map/finish/pallas_call | solution.py:435

commit v6 on v4

--- a/solution.py
+++ b/solution.py
@@ -123,21 +123,34 @@
     def hop(way, step, q):
         return pltpu.make_async_remote_copy(
             src_ref=view(way, step, q), dst_ref=view(way, step, q),
-            send_sem=ring_send.at[way, step, q], recv_sem=ring_recv.at[way, step, q],
+            send_sem=ring_send.at[0], recv_sem=ring_recv.at[way, step, q],
             device_id=neighbour[way], device_id_type=MESH,
         )
 
     def share(way, step, q):
         return pltpu.make_async_remote_copy(
             src_ref=view(way, step, q), dst_ref=view(way, step, q),
-            send_sem=sib_send.at[way, step, q], recv_sem=sib_recv.at[way, step, q],
+            send_sem=sib_send.at[q // 2], recv_sem=sib_recv.at[q // 2],
+            device_id=sibling, device_id_type=MESH,
+        )
+
+    def all_hops():
+        every = rows.at[pl.ds(0, chips - 1)]
+        return pltpu.make_async_remote_copy(
+            src_ref=every, dst_ref=every, send_sem=ring_send.at[0], recv_sem=sib_recv.at[0],
+            device_id=sibling, device_id_type=MESH,
+        )
+
+    def all_shares(p):
+        every = rows.at[pl.ds(0, chips), :, pl.ds(p * half, half)]
+        return pltpu.make_async_remote_copy(
+            src_ref=every, dst_ref=every, send_sem=sib_send.at[p], recv_sem=sib_recv.at[p],
             device_id=sibling, device_id_type=MESH,
         )
 
     def travels(way, step, q):
         return step < far - 1 or (step == far - 1 and way == q % 2)
 
-    hops, shares = [], [[], []]
     for p in range(2):
         for copy in swaps[p]:
             copy.wait_recv()
@@ -148,10 +161,8 @@
             rows[me, :, pl.ds(q * quarter, quarter)] = jnp.concatenate(own, axis=0).astype(BF16)
             for way in range(2):
                 if travels(way, 0, q):
-                    hops.append(hop(way, 0, q))
-                    hops[-1].start()
-            shares[p].append(share(0, 0, q))
-            shares[p][-1].start()
+                    hop(way, 0, q).start()
+            share(0, 0, q).start()
 
     columns = window * 2 * kept
     place = lax.broadcasted_iota(jnp.int32, (columns, 1), 0)
@@ -168,10 +179,8 @@
                 if travels(way, step, q):
                     hop(way, step, q).wait_recv()
                     if travels(way, step + 1, q):
-                        hops.append(hop(way, step + 1, q))
-                        hops[-1].start()
-                    shares[q // 2].append(share(way, step + 1, q))
-                    shares[q // 2][-1].start()
+                        hop(way, step + 1, q).start()
+                    share(way, step + 1, q).start()
     for copy in loads:
         copy.wait()
 
@@ -220,11 +229,9 @@
         lax.fori_loop(0, hidden // tall, pointwise, 0)
         return carry
 
-    for copy in shares[0]:
-        copy.wait_recv()
+    all_shares(0).wait_recv()
     lax.fori_loop(0, total // wide, first_half, 0)
-    for copy in shares[1]:
-        copy.wait_recv()
+    all_shares(1).wait_recv()
     lax.fori_loop(0, total // wide, products, 0)
 
     ordinal = lax.broadcasted_iota(jnp.int32, (n_dp * kept, 1), 0)
@@ -256,7 +263,7 @@
         k = chip_at(spot + offset)
         return pltpu.make_async_remote_copy(
             src_ref=part.at[(1 - core) * chips + k, :, lanes_of(h)], dst_ref=sib.at[k, :, lanes_of(h)],
-            send_sem=pair_send.at[offset, h], recv_sem=pair_recv.at[offset, h],
+            send_sem=pair_send.at[0], recv_sem=pair_recv.at[offset, h],
             device_id=sibling, device_id_type=MESH,
         )
 
@@ -340,10 +347,15 @@
             ))
             returns[-1].start()
     gradients(marks[far], strips)
-    for copy in swaps[0] + swaps[1] + hops + shares[0] + shares[1]:
+    for copy in swaps[0] + swaps[1]:
         copy.wait_send()
-    for copy in pairs.values():
-        copy.wait_send()
+    all_hops().wait_send()
+    for p in range(2):
+        all_shares(p).wait_send()
+    pltpu.make_async_remote_copy(
+        src_ref=part.at[pl.ds(0, chips)], dst_ref=sib, send_sem=pair_send.at[0], recv_sem=pair_recv.at[0, 0],
+        device_id=sibling, device_id_type=MESH,
+    ).wait_send()
     for key in sums:
         rs(*key).wait_send()
     for copy in returns:
@@ -416,11 +428,11 @@
             dma((3,)),
             dma((window, 2)),
             dma((window, 2)),
+            dma((1,)),
             dma((2, far, 4)),
-            dma((2, far, 4)),
-            dma((2, far + 1, 4)),
-            dma((2, far + 1, 4)),
-            dma((chips, 2)),
+            dma((2,)),
+            dma((2,)),
+            dma((1,)),
             dma((chips, 2)),
             dma((2, far, 2)),
             dma((2, far, 2)),

time: 51.3 us -> 50.2 us (0.979)
  Pallas kernels: 50.5 us -> 49.4 us
    pallas_call x1, Pallas kernels: 46.4 us -> 45.2 us  [shards(): pl.pallas_call(functools.partial(exchange_kernel, n_dp, window), out_shap...]
where the time goes in v6:
time: 50.2 us; the launch traced here: 50.1 us
  Pallas kernels  49.4 us (98%)
  between operations  0.64 us (1%)
    pallas_call x1, Pallas kernels, shards(): pl.pallas_call(functools.partial(exchange_kernel, n_dp, window), out_shap...  45.2 us
    pallas_call x1, Pallas kernels, shards(): pl.pallas_call(functools.partial(finish_kernel, hidden), out_shape=(jax.S...  4.18 us

profile of v6, /device:TPU:0, one launch (start us, length us, event | category | flops | bytes accessed | tf_op | source)
XLA Modules:
  0.0 50.1 jit_solution(659061520184363658)
XLA Ops:
  0.6 45.2 %exchange.1 = (bf16[1344,3584]{1,0:T(8,128)(2,1)S(1)}, bf16[2,16,1792]{2,1,0:T(8,128)(2,1)S(1)}, bf16[2,128,32]{2,1,0:T(8,128)(2,1)S(1)}) custom-call(bf16[128,3584]{1,0:T(8,128)(2,1)} %tokens_in.1, bf16[128,3584]{1,0:T(8,128)(2,1)} %cotangent_in.1, s32[2,128]{1,0:T(2,128)} %bitcast.14, f32[2,128]{1,0:T(2,128)} %bitcast.15, bf16[448,3584]{1,0:T(8,128)(2,1)} %bitcast.8, ...), custom_call_target="tpu_custom_call" | custom-call | flops 4110417920 | bytes 13303808 | tf_op jit(solution)/shard_map/exchange/pallas_call | solution.py:403
  45.9 4.2 %finish.1 = (bf16[128,3584]{1,0:T(8,128)(2,1)}, bf16[448,3584]{1,0:T(8,128)(2,1)}, bf16[448,3584]{1,0:T(8,128)(2,1)}, bf16[448,3584]{1,0:T(8,128)(2,1)}) custom-call(bf16[1344,3584]{1,0:T(8,128)(2,1)S(1)} %get-tuple-element.11.grads, bf16[2,16,1792]{2,1,0:T(8,128)(2,1)S(1)} %get-tuple-element.12.back, bf16[2,128,32]{2,1,0:T(8,128)(2,1)S(1)} %get-tuple-element.13.pick), custom_call_target="tpu_custom_call" | custom-call | flops 29360128 | bytes 10551296 | tf_op jit(solution)/shard_map/finish/pallas_call | solution.py:455

commit v7 on v6

--- a/solution.py
+++ b/solution.py
@@ -30,7 +30,7 @@
     n_dp, window,
     tokens_in, cotangent_in, experts, weights, w_gate, w_up, w_down,
     grads_out, back_out, pick_out,
-    tokens, cotangent, returned, d_out, w, sent, arrived, rows, prod, d_rows, part, sib, out_buf, in_buf,
+    select, tokens, cotangent, returned, d_out, w, sent, arrived, rows, prod, d_rows, part, sib, out_buf, in_buf,
     in_sem, w_sem, y_send, y_recv, ring_send, ring_recv, sib_send, sib_recv,
     pair_send, pair_recv, rs_send, rs_recv, z_send, z_recv,
 ):
@@ -51,15 +51,17 @@
     chip = lax.div(me, 2)
     spot = jnp.where(lax.rem(chip, 2) == 0, lax.div(chip, 2), chips - 1 - lax.div(chip, 2))
 
-    def chip_at(place):
-        place = lax.rem(place + 2 * chips, chips)
-        return jnp.where(place < far, 2 * place, 2 * (chips - 1 - place) + 1)
-
-    def at(place):
-        return 2 * chip_at(place) + core
+    ring = []
+    for offset in range(chips):
+        place = spot + offset
+        place = jnp.where(place >= chips, place - chips, place)
+        ring.append(jnp.where(place < far, 2 * place, 2 * (chips - 1 - place) + 1))
+
+    def at(offset):
+        return 2 * ring[offset % chips] + core
 
     sibling = (2 * chip + 1 - core, mine)
-    neighbour = ((at(spot + 1), mine), (at(spot - 1), mine))
+    neighbour = ((at(1), mine), (at(-1), mine))
 
     inputs = []
     for p in range(2):
@@ -117,19 +119,21 @@
         loads[-1].start()
 
     def view(way, step, q):
-        origin = at(spot - step) if way == 0 else at(spot + step)
+        origin = at(-step) if way == 0 else at(step)
         return rows.at[origin, :, pl.ds(q * quarter, quarter)]
 
     def hop(way, step, q):
-        return pltpu.make_async_remote_copy(
-            src_ref=view(way, step, q), dst_ref=view(way, step, q),
+        piece = view(way, step, q)
+        return pltpu.make_async_remote_copy(
+            src_ref=piece, dst_ref=piece,
             send_sem=ring_send.at[0], recv_sem=ring_recv.at[way, step, q],
             device_id=neighbour[way], device_id_type=MESH,
         )
 
     def share(way, step, q):
-        return pltpu.make_async_remote_copy(
-            src_ref=view(way, step, q), dst_ref=view(way, step, q),
+        piece = view(way, step, q)
+        return pltpu.make_async_remote_copy(
+            src_ref=piece, dst_ref=piece,
             send_sem=sib_send.at[q // 2], recv_sem=sib_recv.at[q // 2],
             device_id=sibling, device_id_type=MESH,
         )
@@ -173,6 +177,11 @@
     for h in range(2):
         pick_out[h] = jnp.where(side == h, match, 0.0).astype(BF16)
 
+    ordinal = lax.broadcasted_iota(jnp.int32, (n_dp * kept, 1), 0)
+    owner = 2 * lax.rem(lax.div(ordinal, kept), chips) + lax.div(ordinal, kept * chips)
+    slot = lax.rem(ordinal, kept)
+    select[...] = owner * block + lax.div(slot, CAP) * group + lax.rem(slot, CAP)
+
     for step in range(far):
         for q in range(4):
             for way in range(2):
@@ -187,7 +196,7 @@
     wide = 256 if total % 256 == 0 else total
     blocks = wide // block
     tall = 112 if hidden % 112 == 0 else 16
-    x_lane = lax.rem(lax.broadcasted_iota(jnp.int32, (tall, wide), 1), group) < CAP
+    x_lane = (lax.broadcasted_iota(jnp.int32, (tall, wide), 1) & (group - 1)) < CAP
 
     def multiply(n, h):
         def matrix(index, carry):
@@ -234,13 +243,9 @@
     all_shares(1).wait_recv()
     lax.fori_loop(0, total // wide, products, 0)
 
-    ordinal = lax.broadcasted_iota(jnp.int32, (n_dp * kept, 1), 0)
-    owner = 2 * lax.rem(lax.div(ordinal, kept), chips) + lax.div(ordinal, kept * chips)
-    slot = lax.rem(ordinal, kept)
-    source = owner * block + lax.div(slot, CAP) * group + lax.rem(slot, CAP)
-    select = lax.broadcasted_iota(jnp.int32, (n_dp * kept, total), 1) == source
+    chosen = lax.broadcasted_iota(jnp.int32, (n_dp * kept, total), 1) == select[...]
     d_rows[...] = lax.dot_general(
-        jnp.where(select, 1.0, 0.0).astype(BF16), d_out[pl.ds(0, 2 * hidden), :], NT, preferred_element_type=F32
+        jnp.where(chosen, 1.0, 0.0).astype(BF16), d_out[pl.ds(0, 2 * hidden), :], NT, preferred_element_type=F32
     ).astype(BF16)
     narrow = 256
     chunks = half // narrow
@@ -260,7 +265,7 @@
         return carry
 
     def pair(offset, h):
-        k = chip_at(spot + offset)
+        k = ring[offset]
         return pltpu.make_async_remote_copy(
             src_ref=part.at[(1 - core) * chips + k, :, lanes_of(h)], dst_ref=sib.at[k, :, lanes_of(h)],
             send_sem=pair_send.at[0], recv_sem=pair_recv.at[offset, h],
@@ -320,7 +325,7 @@
                 if (offset, h) not in ready:
                     pairs[offset, h].wait_recv()
                     ready.add((offset, h))
-                k = chip_at(spot + offset)
+                k = ring[offset]
                 value = part[core * chips + k, :, cols].astype(F32) + sib[k, :, cols].astype(F32)
                 if step > 0 and begins(way, step - 1, h):
                     rs(way, step - 1, h).wait_recv()
@@ -410,6 +415,7 @@
         in_specs=[anywhere] * 2 + [vmem] * 2 + [anywhere] * 3,
         out_specs=(vmem, vmem, vmem),
         scratch_shapes=[
+            pltpu.VMEM((n_dp * kept, 1), jnp.int32),
             pltpu.VMEM((count, width), BF16),
             pltpu.VMEM((count, width), BF16),
             pltpu.VMEM((window, block, half), BF16),

time: 50.2 us -> 50.2 us (level)
  no operation moved by 1% of the time
where the time goes in v7:
time: 50.2 us; the launch traced here: 50.1 us
  Pallas kernels  49.4 us (98%)
  between operations  0.64 us (1%)
    pallas_call x1, Pallas kernels, shards(): pl.pallas_call(functools.partial(exchange_kernel, n_dp, window), out_shap...  45.2 us
    pallas_call x1, Pallas kernels, shards(): pl.pallas_call(functools.partial(finish_kernel, hidden), out_shape=(jax.S...  4.18 us

profile of v7, /device:TPU:0, one launch (start us, length us, event | category | flops | bytes accessed | tf_op | source)
XLA Modules:
  0.0 50.1 jit_solution(9647852189430218772)
XLA Ops:
  0.6 45.2 %exchange.1 = (bf16[1344,3584]{1,0:T(8,128)(2,1)S(1)}, bf16[2,16,1792]{2,1,0:T(8,128)(2,1)S(1)}, bf16[2,128,32]{2,1,0:T(8,128)(2,1)S(1)}) custom-call(bf16[128,3584]{1,0:T(8,128)(2,1)} %tokens_in.1, bf16[128,3584]{1,0:T(8,128)(2,1)} %cotangent_in.1, s32[2,128]{1,0:T(2,128)} %bitcast.14, f32[2,128]{1,0:T(2,128)} %bitcast.15, bf16[448,3584]{1,0:T(8,128)(2,1)} %bitcast.8, ...), custom_call_target="tpu_custom_call" | custom-call | flops 4110417920 | bytes 13303808 | tf_op jit(solution)/shard_map/exchange/pallas_call | solution.py:408
  45.9 4.2 %finish.1 = (bf16[128,3584]{1,0:T(8,128)(2,1)}, bf16[448,3584]{1,0:T(8,128)(2,1)}, bf16[448,3584]{1,0:T(8,128)(2,1)}, bf16[448,3584]{1,0:T(8,128)(2,1)}) custom-call(bf16[1344,3584]{1,0:T(8,128)(2,1)S(1)} %get-tuple-element.11.grads, bf16[2,16,1792]{2,1,0:T(8,128)(2,1)S(1)} %get-tuple-element.12.back, bf16[2,128,32]{2,1,0:T(8,128)(2,1)S(1)} %get-tuple-element.13.pick), custom_call_target="tpu_custom_call" | custom-call | flops 29360128 | bytes 10551296 | tf_op jit(solution)/shard_map/finish/pallas_call | solution.py:461
